TPU v7x, 512 devices: a whole 4x4x16 slice. The times are simulated.
512 devices in a mesh: env: 64 (over z_lo, x, core), sp: 8 (over y, z_hi).
Axes of the slice: x: 4, y: 4, z: 16 (z_hi: 2, z_lo: 8; z = z_hi * 8 + z_lo), core: 2. Of those that a mesh axis runs over, the one named last changes fastest.
Arguments:
- descriptors: bfloat16 [98304, 1024], P('env'), may hold values from -6 to 6
- env_species: int32 [98304], P('env'), may hold values from 0 to 3
- structure: int32 [64, 1536], P('env'), may hold values from 0 to 23, never falling along the last dimension, each value on 1 to 128 neighbouring positions
- energies: float32 [1536], P('env'), may hold values from -6 to 6
- sparse_points: bfloat16 [4096, 1024], P('sp'), may hold values from -6 to 6
- sparse_species: int32 [4096], P('sp'), may hold values from 0 to 3
Outputs:
- gram: float32 [4096, 4096], P('sp', 'env')
- fit_rhs: float32 [4096], P('sp')
Inputs may be any that keep to these rules, and one draw needn't show every extreme that they name: Each row numbers the structures of one index of env from 0 to 23 in order, never falling; each structure has 1 to 128 environments and some has exactly 128.
All inputs are finite; a program needn't handle non-finite values.
Results may differ from a plain program's by a relative error of at most 0.0003.
Values sent between devices are 32-bit elements; how exact they have to be, the bound alone decides.
No kernel may reach another device: no remote copies, remote signals or barrier semaphores. Data moves between devices by JAX's collectives and lax.ppermute only.
A program may use at most 64 MiB of HBM per device.

v0:
```python
import math

import jax
import jax.numpy as jnp
from jax import lax
from jax.sharding import PartitionSpec as P

D = 1024


def spread(block, axis, source):
    block = jnp.where(lax.axis_index(axis) == source, block, jnp.zeros_like(block))
    return lax.psum(block, axis)


def weigh_columns(descriptors, env_kinds, points, point_kinds, onehot, factor):
    scale = 1.0 / math.sqrt(D)
    dots = (
        lax.dot_general(
            descriptors, points, (((1,), (1,)), ((), ())), preferred_element_type=jnp.float32
        )
        * scale
    )
    squares = dots * dots
    kernel = squares * squares * (env_kinds[:, None] == point_kinds[None, :]).astype(jnp.float32)
    summed = jnp.dot(
        onehot, kernel, precision=lax.Precision.HIGHEST, preferred_element_type=jnp.float32
    )
    return summed * factor[:, None]


def local(descriptors, env_species, structure, energies, sparse_points, sparse_species):
    env_count = lax.axis_size("env")
    sp_count = lax.axis_size("sp")
    str_local = energies.shape[0]
    cols_local = sparse_points.shape[0]
    total_structs = str_local * env_count
    total_sparse = cols_local * sp_count
    owned = total_sparse // env_count
    labels = structure[0]
    onehot = (jnp.arange(str_local, dtype=jnp.int32)[:, None] == labels[None, :]).astype(
        jnp.float32
    )
    counts = jnp.sum(onehot, axis=1)
    factor = 1.0 / math.sqrt(total_structs) / counts
    first_col = lax.axis_index("env") * owned
    owner_index = first_col // cols_local
    offset = jnp.clip(first_col - lax.axis_index("sp") * cols_local, 0, cols_local - owned)
    weighted = weigh_columns(
        descriptors, env_species, sparse_points, sparse_species, onehot, factor
    )
    all_rows = lax.all_gather(weighted, "env", axis=0, tiled=True)
    partial_rhs = jnp.dot(
        energies, weighted, precision=lax.Precision.HIGHEST, preferred_element_type=jnp.float32
    )
    fit_rhs = lax.psum(partial_rhs, "env")
    piece = lax.dynamic_slice_in_dim(all_rows, offset, owned, 1)
    slab = spread(piece, "sp", owner_index)
    gram = lax.dot_general(
        all_rows,
        slab,
        (((0,), (0,)), ((), ())),
        precision=lax.Precision.HIGHEST,
        preferred_element_type=jnp.float32,
    )
    return (gram, fit_rhs)


def solution(mesh):
    in_specs = (P("env", None), P("env"), P("env", None), P("env"), P("sp", None), P("sp"))
    out_specs = (P("sp", "env"), P("sp"))
    return jax.shard_map(local, mesh=mesh, in_specs=in_specs, out_specs=out_specs, check_vma=False)
```

profile of v0, /device:TPU:8, one launch (start us, length us, event | category | flops | bytes accessed | tf_op | source)
XLA Modules:
  0.0 391.9 jit_solution(2968505812892047556)
XLA Ops:
  7.2 0.0 copy-start
  7.2 0.0 all-gather.2.cloned.1.call-start
  7.2 0.9 reduce
  8.1 0.1 convert_reduce_fusion
  8.2 0.8 copy-done
  9.1 3.3 fusion.2
  12.4 0.0 copy-start.1
  12.4 1.8 convolution_multiply_fusion.1
  14.2 0.0 all-gather.2.cloned.1.call-update
  14.2 0.0 all-reduce.2.cloned.1.call-start
  14.3 126.5 %all-gather.2.cloned.1.call-done = f32[1536,512]{1,0:T(8,128)} async-done(((f32[24,512]{1,0:T(8,128)}), f32[1536,512]{1,0:T(8,128)}) %all-gather.2.cloned.1.call-update) | async-done | bytes 3145744 | tf_op jit(solution)/shard_map/all_gather | solution.py:52
  140.8 2.6 dynamic-slice_select_fusion
  143.4 0.0 all-reduce.2.cloned.1.call-update
  143.4 0.0 copy-done.1
  143.4 1.0 fusion.4
  144.4 236.0 %psum.15 = f32[512]{0:T(512)} all-reduce(f32[512]{0:T(512)S(1)} %bitcast.10), channel_id=1, replica_groups=mesh['env'=64,'sp'=8] {'env'}, use_global_device_ids=true, to_apply=%region_2.3 | all-reduce | flops 512 | bytes 4096 | tf_op jit(solution)/shard_map/psum | solution.py:56
  380.4 0.0 all-reduce.2.cloned.1.call-done
  380.4 4.6 %fusion.6 = f32[512,64]{0,1:T(8,128)} fusion(f32[1536,512]{1,0:T(8,128)} %all-gather.2.cloned.1.call-done, f32[1536,64]{1,0:T(8,128)} %all-reduce.2.cloned.1.call-done), kind=kOutput, calls=%fused_computation.12 | convolution fusion | flops 603979776 | bytes 3670016 | tf_op jit(solution)/shard_map/dot_general | solution.py:59
  (1 shorter events, 0.0 us)
Async XLA Ops:
  7.2 1.9 copy-start
  7.2 133.6 %all-gather.2.cloned.1.call-start = ((), (), s32[]{:S(2)}) async-start(), calls=%async_computation | async-start | bytes 3194880 | tf_op jit(solution)/shard_map/all_gather | solution.py:52
  12.4 131.0 %copy-start.1 = (f32[24]{0:T(128)S(1)}, f32[24]{0:T(128)}, u32[]{:S(2)}) copy-start(f32[24]{0:T(128)} %param.9) | copy-start | bytes 292
  14.2 366.2 %all-reduce.2.cloned.1.call-start = ((), (), s32[]{:S(2)}) async-start(), calls=%async_computation.1 | async-start | bytes 1572864 | tf_op jit(solution)/shard_map/psum | solution.py:13
Sparse Core Ops, SparseCore 0:
  14.3 126.4 all-gather.1
  143.8 203.5 all-reduce.1
where the time goes:
time: 392 us
  blocking collectives  236 us (60%)
  waiting for transfers between devices  127 us (32%)
  between operations  14.1 us (4%)
  matrix products  10.7 us (3%)
    psum x1, blocking collectives, local(): fit_rhs = lax.psum(partial_rhs, 'env')  236 us
    all_gather x1, waiting for transfers between devices, local(): all_rows = lax.all_gather(weighted, 'env', axis=0, tiled=True)  127 us
  transfers between devices with their start and end apart: 2, of which 1 were waited for; matrix products, arithmetic and copies ran while one was open for 0% of the time, Pallas kernels for 0%

commit v1 on v0

v1 whole, which is shorter than its diff:
```python
import math

import jax
import jax.numpy as jnp
from jax import lax
from jax.sharding import PartitionSpec as P

D = 1024
AXES = ("env", "sp")
ZL, X, C, Y, ZH = 8, 4, 2, 4, 2


def pairs(move):
    out = []
    for zl in range(ZL):
        for x in range(X):
            for c in range(C):
                for y in range(Y):
                    for zh in range(ZH):
                        a, b, d, e, f = move(zl, x, c, y, zh)
                        here = (((zl * X + x) * C + c) * Y + y) * ZH + zh
                        there = (((a * X + b) * C + d) * Y + e) * ZH + f
                        out.append((here, there))
    return out


def send(value, move):
    return lax.ppermute(value, AXES, pairs(move))


def over_z(m):
    return lambda zl, x, c, y, zh: (zl ^ m, x, c, y, zh)


def over_y(m):
    return lambda zl, x, c, y, zh: (zl, x, c, y ^ m, zh)


def over_x(m):
    return lambda zl, x, c, y, zh: (zl, x ^ m, c, y, zh)


def over_core(zl, x, c, y, zh):
    return (zl, x, 1 - c, y, zh)


def turned(flip):
    return lambda zl, x, c, y, zh: (y * ZH + zh, x, c, zl // ZH, (zl % ZH) ^ flip)


def weigh_columns(descriptors, env_kinds, points, point_kinds, onehot, factor):
    scale = 1.0 / math.sqrt(D)
    dots = (
        lax.dot_general(
            descriptors, points, (((1,), (1,)), ((), ())), preferred_element_type=jnp.float32
        )
        * scale
    )
    squares = dots * dots
    kernel = squares * squares * (env_kinds[:, None] == point_kinds[None, :]).astype(jnp.float32)
    summed = jnp.dot(
        onehot, kernel, precision=lax.Precision.HIGHEST, preferred_element_type=jnp.float32
    )
    return summed * factor[:, None]


def local(descriptors, env_species, structure, energies, sparse_points, sparse_species):
    str_local = energies.shape[0]
    cols = sparse_points.shape[0]
    total_structs = str_local * ZL * X * C
    owned = cols // (X * C)
    labels = structure[0]
    onehot = (jnp.arange(str_local, dtype=jnp.int32)[:, None] == labels[None, :]).astype(
        jnp.float32
    )
    counts = jnp.sum(onehot, axis=1)
    factor = 1.0 / math.sqrt(total_structs) / counts
    weighted = weigh_columns(
        descriptors, env_species, sparse_points, sparse_species, onehot, factor
    )
    rhs = jnp.dot(
        energies[None], weighted, precision=lax.Precision.HIGHEST, preferred_element_type=jnp.float32
    )
    env, sp = lax.axis_index("env"), lax.axis_index("sp")
    zl, c, x = env // (X * C), env % C, env // C % X

    lanes = cols // 4
    cut = weighted.reshape(str_local, 4, lanes).transpose(1, 0, 2).reshape(4 * str_local, lanes)
    tail = jnp.concatenate([rhs.reshape(4, lanes), jnp.zeros((4, lanes), jnp.float32)])
    wire = jnp.concatenate([cut, tail])

    far = send(wire, over_z(4))
    t0 = send(cut, turned(0))
    t1 = send(cut, turned(1))
    pair = jnp.stack([wire, far])
    near = [pair] + [send(pair, over_z(m)) for m in (1, 2, 3)]
    mine = jnp.stack([t0, t1])
    across = [mine] + [send(mine, over_y(m)) for m in (1, 2, 3)]

    a_blocks = jnp.stack([b[h] for h in (0, 1) for b in near])
    rhs_sum = jnp.sum(a_blocks[:, 4 * str_local : 4 * str_local + 4], axis=0).reshape(1, cols)
    b_blocks = jnp.stack([b[f] for b in across for f in (0, 1)])
    order = jnp.arange(8) ^ zl ^ sp
    b_blocks = jnp.take(b_blocks, order, axis=0)

    def rows(blocks):
        return (
            blocks[:, : 4 * str_local]
            .reshape(8, 4, str_local, lanes)
            .transpose(0, 2, 1, 3)
            .reshape(8 * str_local, cols)
        )

    tile = lax.dot_general(
        rows(b_blocks),
        rows(a_blocks),
        (((0,), (0,)), ((), ())),
        precision=lax.Precision.HIGHEST,
        preferred_element_type=jnp.float32,
    )
    tile = tile.reshape(X, C, owned, cols)
    keep = lax.dynamic_index_in_dim(tile, c, 1, keepdims=False)
    give = lax.dynamic_index_in_dim(tile, 1 - c, 1, keepdims=False)
    line = jnp.concatenate([rhs_sum, jnp.zeros((7, cols), jnp.float32)])
    payload = jnp.concatenate([give.reshape(X * owned, cols), line])
    got = send(payload, over_core)
    keep = keep + got[: X * owned].reshape(X, owned, cols)
    line = line + got[X * owned :]
    parts = [
        send(
            jnp.concatenate([lax.dynamic_index_in_dim(keep, x ^ m, 0, keepdims=False), line]),
            over_x(m),
        )
        for m in (2, 1, 3)
    ]
    total = (
        jnp.concatenate([lax.dynamic_index_in_dim(keep, x, 0, keepdims=False), line])
        + parts[0]
        + (parts[1] + parts[2])
    )
    return total[:owned].T, total[owned]


def solution(mesh):
    in_specs = (P("env", None), P("env"), P("env", None), P("env"), P("sp", None), P("sp"))
    out_specs = (P("sp", "env"), P("sp"))
    return jax.shard_map(local, mesh=mesh, in_specs=in_specs, out_specs=out_specs, check_vma=False)
```

time: 392 us -> 106 us (0.27)
  the two profiles are of different devices: /device:TPU:8 before, /device:TPU:1 now
where the time goes in v1:
time: 106 us; the launch traced here: 104 us
  starting transfers between devices  61.3 us (58%)
  local copies, waits for them, and re-layouts  22.4 us (21%)
  waiting for transfers between devices  6.89 us (6%)
  matrix products  6.81 us (6%)
  other arithmetic  6.19 us (6%)
    ppermute x13, starting transfers between devices, send(): return lax.ppermute(value, AXES, pairs(move))  61.3 us
    unnamed x19, local copies, waits for them, and re-layouts  13 us
    ppermute x13, waiting for transfers between devices, send(): return lax.ppermute(value, AXES, pairs(move))  6.89 us
    dot_general x1, matrix products, weigh_columns(): lax.dot_general(descriptors, points, (((1,), (1,)), ((), ())), preferred_...  3.39 us
    dot_general x1, matrix products, local(): lax.dot_general(rows(b_blocks), rows(a_blocks), (((0,), (0,)), ((), ())),...  2.15 us
  transfers between devices with their start and end apart: 13, of which 3 were waited for; matrix products, arithmetic and copies ran while one was open for 10% of the time, Pallas kernels for 0%

profile of v1, /device:TPU:1, one launch (start us, length us, event | category | flops | bytes accessed | tf_op | source)
XLA Modules:
  0.0 104.5 jit_solution(16624730112016248735)
XLA Ops:
  0.6 0.0 copy-start
  0.6 0.9 reduce
  1.5 0.1 convert_reduce_fusion
  1.6 0.9 copy-done
  2.5 3.4 %fusion.2 = f32[1536,512]{1,0:T(8,128)S(1)} fusion(bf16[1536,1024]{1,0:T(8,128)(2,1)S(1)} %copy-done, bf16[512,1024]{1,0:T(8,128)(2,1)} %param.10, s32[512]{0:T(512)} %param.11, s32[1536]{0:T(1024)} %param.7), kind=kOutput, calls=%fused_computation.4 | convolution fusion | flops 1614544896 | bytes 7348224 | tf_op jit(solution)/shard_map/dot_general | solution.py:54
  5.9 0.0 copy-start.3
  5.9 1.1 %fusion.3 = f32[3,4,8,128]{3,2,1,0:T(8,128)S(1)} fusion(f32[1536,512]{1,0:T(8,128)S(1)} %fusion.2, s32[1536]{0:T(1024)S(1)} %reduce, f32[24]{0:T(128)S(1)} %broadcast_divide_fusion), kind=kOutput, calls=%fused_computation.6 | convolution fusion | flops 226541568 | bytes 3201120 | tf_op jit(solution)/shard_map/dot_general | solution.py:61
  7.1 0.7 collective-permute-start
  7.8 17.5 %collective-permute-start.1 = (f32[96,128]{1,0:T(8,128)S(1)}, f32[96,128]{1,0:T(8,128)S(1)}, u32[]{:S(2)}, u32[]{:S(2)}) collective-permute-start(f32[96,128]{1,0:T(8,128)S(1)} %bitcast.75), channel_id=1, source_target_pairs={{0,1},{1,65},{2,129},{3,193},{4,257},{5,321},{6,385},{7,449},{8,9}... | collective-permute-start | bytes 147464 | tf_op jit(solution)/shard_map/ppermute | solution.py:28
  25.3 0.1 fusion.9
  25.5 0.1 pad.16.clone
  25.5 0.1 fusion.14
  25.6 4.8 %collective-permute-start.5 = (f32[104,128]{1,0:T(8,128)S(1)}, f32[104,128]{1,0:T(8,128)S(1)}, u32[]{:S(2)}, u32[]{:S(2)}) collective-permute-start(f32[104,128]{1,0:T(8,128)S(1)} %get-tuple-element.7), channel_id=1, source_target_pairs={{0,256},{1,257},{2,258},{3,259},{4,260},{5,261},{6,262},{7,263},{8... | collective-permute-start | bytes 159752 | tf_op jit(solution)/shard_map/ppermute | solution.py:28
  30.5 0.7 constant_dynamic-update-slice_fusion.6
  31.2 0.1 pad.11.clone
  31.3 0.0 collective-permute-done
  31.3 0.0 collective-permute-done.1
  31.3 2.5 %collective-permute-start.2 = (f32[2,96,128]{2,1,0:T(8,128)S(1)}, f32[2,96,128]{2,1,0:T(8,128)S(1)}, u32[]{:S(2)}, u32[]{:S(2)}) collective-permute-start(f32[2,96,128]{2,1,0:T(8,128)S(1)} %pad_maximum_fusion.5), channel_id=1, source_target_pairs={{0,2},{1,3},{2,0},{3,1},{4,6},{5,7},{6,4},{7,5},{8,10},{9,11},{10,... | collective-permute-start | bytes 294920 | tf_op jit(solution)/shard_map/ppermute | solution.py:28
  33.8 6.6 %collective-permute-start.3 = (f32[2,96,128]{2,1,0:T(8,128)S(1)}, f32[2,96,128]{2,1,0:T(8,128)S(1)}, u32[]{:S(2)}, u32[]{:S(2)}) collective-permute-start(f32[2,96,128]{2,1,0:T(8,128)S(1)} %pad_maximum_fusion.5), channel_id=1, source_target_pairs={{0,4},{1,5},{2,6},{3,7},{4,0},{5,1},{6,2},{7,3},{8,12},{9,13},{10,... | collective-permute-start | bytes 294920 | tf_op jit(solution)/shard_map/ppermute | solution.py:28
  40.4 1.9 %collective-permute-start.4 = (f32[2,96,128]{2,1,0:T(8,128)S(1)}, f32[2,96,128]{2,1,0:T(8,128)S(1)}, u32[]{:S(2)}, u32[]{:S(2)}) collective-permute-start(f32[2,96,128]{2,1,0:T(8,128)S(1)} %pad_maximum_fusion.5), channel_id=1, source_target_pairs={{0,6},{1,7},{2,4},{3,5},{4,2},{5,3},{6,0},{7,1},{8,14},{9,15},{10,... | collective-permute-start | bytes 294920 | tf_op jit(solution)/shard_map/ppermute | solution.py:28
  42.4 0.6 constant_dynamic-update-slice_fusion.4
  43.0 0.6 constant_dynamic-update-slice_fusion.3
  43.6 0.0 collective-permute-done.5
  43.6 0.7 pad_maximum_fusion.4
  44.3 6.6 %collective-permute-start.6 = (f32[2,104,128]{2,1,0:T(8,128)}, f32[2,104,128]{2,1,0:T(8,128)}, u32[]{:S(2)}, u32[]{:S(2)}) collective-permute-start(f32[2,104,128]{2,1,0:T(8,128)} %pad_maximum_fusion.4), channel_id=1, source_target_pairs={{0,64},{1,65},{2,66},{3,67},{4,68},{5,69},{6,70},{7,71},{8,72},{9,... | collective-permute-start | bytes 319496 | tf_op jit(solution)/shard_map/ppermute | solution.py:28
  50.9 3.3 %collective-permute-start.7 = (f32[2,104,128]{2,1,0:T(8,128)}, f32[2,104,128]{2,1,0:T(8,128)}, u32[]{:S(2)}, u32[]{:S(2)}) collective-permute-start(f32[2,104,128]{2,1,0:T(8,128)} %pad_maximum_fusion.4), channel_id=1, source_target_pairs={{0,128},{1,129},{2,130},{3,131},{4,132},{5,133},{6,134},{7,135},{8... | collective-permute-start | bytes 319496 | tf_op jit(solution)/shard_map/ppermute | solution.py:28
  54.2 0.0 collective-permute-done.2
  54.2 2.6 %collective-permute-start.8 = (f32[2,104,128]{2,1,0:T(8,128)}, f32[2,104,128]{2,1,0:T(8,128)}, u32[]{:S(2)}, u32[]{:S(2)}) collective-permute-start(f32[2,104,128]{2,1,0:T(8,128)} %pad_maximum_fusion.4), channel_id=1, source_target_pairs={{0,192},{1,193},{2,194},{3,195},{4,196},{5,197},{6,198},{7,199},{8... | collective-permute-start | bytes 319496 | tf_op jit(solution)/shard_map/ppermute | solution.py:28
  56.8 0.7 constant_dynamic-update-slice_fusion.2
  57.5 0.0 collective-permute-done.3
  57.5 0.6 constant_dynamic-update-slice_fusion.1
  58.1 0.6 constant_dynamic-update-slice_fusion
  58.7 1.6 %gather_fusion = f32[8,96,128]{2,1,0:T(8,128)S(1)} fusion(f32[8,96,128]{2,1,0:T(8,128)} %constant_dynamic-update-slice_fusion, s32[1024]{0:T(1024)S(1)} %pad_clamp_fusion), kind=kCustom, calls=%fused_computation | custom fusion | bytes 786464 | tf_op jit(solution)/shard_map/jit(_take)/gather | solution.py:104
  60.3 0.1 select_bitcast_fusion
  60.4 0.1 copy.17
  60.6 1.0 copy.18
  61.6 1.4 %slice_dynamic-update-slice_fusion.5 = f32[8,104,128]{2,1,0:T(8,128)} fusion(f32[8,104,128]{2,1,0:T(8,128)} %constant_dynamic-update-slice_fusion.6, f32[2,104,128]{2,1,0:T(8,128)} %collective-permute-done.6), kind=kLoop, calls=%fused_computation.34 | loop fusion | bytes 106496
  63.0 1.4 %slice_dynamic-update-slice_fusion.4 = f32[8,104,128]{2,1,0:T(8,128)} fusion(f32[8,104,128]{2,1,0:T(8,128)} %slice_dynamic-update-slice_fusion.5, f32[2,104,128]{2,1,0:T(8,128)} %collective-permute-done.7), kind=kLoop, calls=%fused_computation.33 | loop fusion | bytes 106496
  64.4 0.0 collective-permute-done.8
  64.4 1.4 %slice_dynamic-update-slice_fusion.3 = f32[8,104,128]{2,1,0:T(8,128)} fusion(f32[8,104,128]{2,1,0:T(8,128)} %slice_dynamic-update-slice_fusion.4, f32[2,104,128]{2,1,0:T(8,128)} %collective-permute-done.8), kind=kLoop, calls=%fused_computation.32 | loop fusion | bytes 106496
  65.9 1.4 %constant_dynamic-update-slice_fusion.5 = f32[8,104,128]{2,1,0:T(8,128)} fusion(f32[8,104,128]{2,1,0:T(8,128)} %slice_dynamic-update-slice_fusion.3, f32[104,128]{1,0:T(8,128)} %copy-done.2), kind=kLoop, calls=%fused_computation.45 | loop fusion | bytes 106496
  67.3 1.4 %slice_dynamic-update-slice_fusion.2 = f32[8,104,128]{2,1,0:T(8,128)} fusion(f32[8,104,128]{2,1,0:T(8,128)} %constant_dynamic-update-slice_fusion.5, f32[2,104,128]{2,1,0:T(8,128)} %collective-permute-done.6), kind=kLoop, calls=%fused_computation.31 | loop fusion | bytes 106496
  68.7 1.4 %slice_dynamic-update-slice_fusion.1 = f32[8,104,128]{2,1,0:T(8,128)} fusion(f32[8,104,128]{2,1,0:T(8,128)} %slice_dynamic-update-slice_fusion.2, f32[2,104,128]{2,1,0:T(8,128)} %collective-permute-done.7), kind=kLoop, calls=%fused_computation.30 | loop fusion | bytes 106496
  70.2 1.4 %slice_dynamic-update-slice_fusion = f32[8,104,128]{2,1,0:T(8,128)} fusion(f32[8,104,128]{2,1,0:T(8,128)} %slice_dynamic-update-slice_fusion.1, f32[2,104,128]{2,1,0:T(8,128)} %collective-permute-done.8), kind=kLoop, calls=%fused_computation.29 | loop fusion | bytes 106496 | tf_op jit(solution)/shard_map/stack | solution.py:100
  71.6 0.8 slice_reduce_fusion
  72.4 1.0 slice.65
  73.4 0.1 copy.19
  73.5 0.9 reshape.86
  74.4 2.1 %fusion.4 = f32[4,2,64,512]{3,2,1,0:T(8,128)S(1)} fusion(f32[4,2,64,192]{3,2,1,0:T(8,128)} %bitcast.67, f32[192,512,1,1]{1,0,2,3:T(8,128)} %reshape.86), kind=kOutput, calls=%fused_computation.10 | convolution fusion | flops 603979776 | bytes 1835008 | tf_op jit(solution)/shard_map/dot_general | solution.py:114
  76.6 1.0 copy-done.1
  77.6 0.9 maximum_maximum_fusion
  78.5 5.4 %collective-permute-start.9 = (f32[264,512]{1,0:T(8,128)}, f32[264,512]{1,0:T(8,128)}, u32[]{:S(2)}, u32[]{:S(2)}) collective-permute-start(f32[264,512]{1,0:T(8,128)} %maximum_maximum_fusion), channel_id=1, source_target_pairs={{0,8},{1,9},{2,10},{3,11},{4,12},{5,13},{6,14},{7,15},{8,0},{9,1},... | collective-permute-start | bytes 1622024 | tf_op jit(solution)/shard_map/ppermute | solution.py:28
  83.9 1.8 %collective-permute-done.9 = f32[264,512]{1,0:T(8,128)} collective-permute-done((f32[264,512]{1,0:T(8,128)}, f32[264,512]{1,0:T(8,128)}, u32[]{:S(2)}, u32[]{:S(2)}) %collective-permute-start.9) | collective-permute-done | bytes 540704 | tf_op jit(solution)/shard_map/ppermute | solution.py:28
  85.8 1.1 %slice.67 = f32[256,512]{1,0:T(8,128)S(1)} slice(f32[264,512]{1,0:T(8,128)} %collective-permute-done.9), slice={[0:256], [0:512]} | slice | bytes 1048576 | tf_op jit(solution)/shard_map/slice | solution.py:127
  86.8 1.1 %bitcast_add_fusion = f32[4,64,512]{2,1,0:T(8,128)S(1)} fusion(f32[4,64,512]{2,1,0:T(8,128)S(1)} %bitcast.69, f32[4,2,64,512]{3,2,1,0:T(8,128)} %copy-done.1, s32[]{:T(128)S(6)} %select_n.64), kind=kLoop, calls=%fused_computation.8 | loop fusion | flops 131072 | bytes 1572868 | tf_op jit(solution)/shard_map/add | solution.py:127
  88.0 0.7 slice_add_fusion
  88.8 4.6 %collective-permute-start.10 = (f32[72,512]{1,0:T(8,128)S(1)}, f32[72,512]{1,0:T(8,128)S(1)}, u32[]{:S(2)}, u32[]{:S(2)}) collective-permute-start(f32[72,512]{1,0:T(8,128)S(1)} %get-tuple-element.9), channel_id=1, source_target_pairs={{0,32},{1,33},{2,34},{3,35},{4,36},{5,37},{6,38},{7,39},{8,40},{9,... | collective-permute-start | bytes 442376 | tf_op jit(solution)/shard_map/ppermute | solution.py:28
  93.4 2.2 %collective-permute-start.11 = (f32[72,512]{1,0:T(8,128)S(1)}, f32[72,512]{1,0:T(8,128)S(1)}, u32[]{:S(2)}, u32[]{:S(2)}) collective-permute-start(f32[72,512]{1,0:T(8,128)S(1)} %get-tuple-element.10), channel_id=1, source_target_pairs={{0,16},{1,17},{2,18},{3,19},{4,20},{5,21},{6,22},{7,23},{8,24},{9,... | collective-permute-start | bytes 442376 | tf_op jit(solution)/shard_map/ppermute | solution.py:28
  95.7 2.5 %collective-permute-start.12 = (f32[72,512]{1,0:T(8,128)S(1)}, f32[72,512]{1,0:T(8,128)S(1)}, u32[]{:S(2)}, u32[]{:S(2)}) collective-permute-start(f32[72,512]{1,0:T(8,128)S(1)} %get-tuple-element.8), channel_id=1, source_target_pairs={{0,48},{1,49},{2,50},{3,51},{4,52},{5,53},{6,54},{7,55},{8,56},{9,... | collective-permute-start | bytes 442376 | tf_op jit(solution)/shard_map/ppermute | solution.py:28
  98.2 0.0 collective-permute-done.10
  98.2 2.1 %collective-permute-done.11 = f32[72,512]{1,0:T(8,128)S(1)} collective-permute-done((f32[72,512]{1,0:T(8,128)S(1)}, f32[72,512]{1,0:T(8,128)S(1)}, u32[]{:S(2)}, u32[]{:S(2)}) %collective-permute-start.11) | collective-permute-done | bytes 147488 | tf_op jit(solution)/shard_map/ppermute | solution.py:28
  100.3 2.9 %collective-permute-done.12 = f32[72,512]{1,0:T(8,128)S(1)} collective-permute-done((f32[72,512]{1,0:T(8,128)S(1)}, f32[72,512]{1,0:T(8,128)S(1)}, u32[]{:S(2)}, u32[]{:S(2)}) %collective-permute-start.12) | collective-permute-done | bytes 147488 | tf_op jit(solution)/shard_map/ppermute | solution.py:28
  103.2 0.7 slice_bitcast_fusion
  103.9 0.6 slice.70
  (20 shorter events, 0.3 us)
Async XLA Ops:
  0.6 1.9 %copy-start = (bf16[1536,1024]{1,0:T(8,128)(2,1)S(1)}, bf16[1536,1024]{1,0:T(8,128)(2,1)}, u32[]{:S(2)}) copy-start(bf16[1536,1024]{1,0:T(8,128)(2,1)} %param.6) | copy-start | bytes 9437188
  5.9 19.4 %copy-start.3 = (f32[24]{0:T(128)S(1)}, f32[24]{0:T(128)}, u32[]{:S(2)}) copy-start(f32[24]{0:T(128)} %param.9) | copy-start | bytes 292
  7.1 24.2 %collective-permute-start = (f32[96,128]{1,0:T(8,128)S(1)}, f32[96,128]{1,0:T(8,128)S(1)}, u32[]{:S(2)}, u32[]{:S(2)}) collective-permute-start(f32[96,128]{1,0:T(8,128)S(1)} %bitcast.74), channel_id=1, source_target_pairs={{0,0},{1,64},{2,128},{3,192},{4,256},{5,320},{6,384},{7,448},{8,8}... | collective-permute-start | bytes 147464 | tf_op jit(solution)/shard_map/ppermute | solution.py:28
  7.8 23.5 %collective-permute-start.1 = (f32[96,128]{1,0:T(8,128)S(1)}, f32[96,128]{1,0:T(8,128)S(1)}, u32[]{:S(2)}, u32[]{:S(2)}) collective-permute-start(f32[96,128]{1,0:T(8,128)S(1)} %bitcast.75), channel_id=1, source_target_pairs={{0,1},{1,65},{2,129},{3,193},{4,257},{5,321},{6,385},{7,449},{8,9}... | collective-permute-start | bytes 147464 | tf_op jit(solution)/shard_map/ppermute | solution.py:28
  25.6 18.0 %collective-permute-start.5 = (f32[104,128]{1,0:T(8,128)S(1)}, f32[104,128]{1,0:T(8,128)S(1)}, u32[]{:S(2)}, u32[]{:S(2)}) collective-permute-start(f32[104,128]{1,0:T(8,128)S(1)} %get-tuple-element.7), channel_id=1, source_target_pairs={{0,256},{1,257},{2,258},{3,259},{4,260},{5,261},{6,262},{7,263},{8... | collective-permute-start | bytes 159752 | tf_op jit(solution)/shard_map/ppermute | solution.py:28
  31.3 22.9 %collective-permute-start.2 = (f32[2,96,128]{2,1,0:T(8,128)S(1)}, f32[2,96,128]{2,1,0:T(8,128)S(1)}, u32[]{:S(2)}, u32[]{:S(2)}) collective-permute-start(f32[2,96,128]{2,1,0:T(8,128)S(1)} %pad_maximum_fusion.5), channel_id=1, source_target_pairs={{0,2},{1,3},{2,0},{3,1},{4,6},{5,7},{6,4},{7,5},{8,10},{9,11},{10,... | collective-permute-start | bytes 294920 | tf_op jit(solution)/shard_map/ppermute | solution.py:28
  33.8 23.6 %collective-permute-start.3 = (f32[2,96,128]{2,1,0:T(8,128)S(1)}, f32[2,96,128]{2,1,0:T(8,128)S(1)}, u32[]{:S(2)}, u32[]{:S(2)}) collective-permute-start(f32[2,96,128]{2,1,0:T(8,128)S(1)} %pad_maximum_fusion.5), channel_id=1, source_target_pairs={{0,4},{1,5},{2,6},{3,7},{4,0},{5,1},{6,2},{7,3},{8,12},{9,13},{10,... | collective-permute-start | bytes 294920 | tf_op jit(solution)/shard_map/ppermute | solution.py:28
  40.4 17.7 %collective-permute-start.4 = (f32[2,96,128]{2,1,0:T(8,128)S(1)}, f32[2,96,128]{2,1,0:T(8,128)S(1)}, u32[]{:S(2)}, u32[]{:S(2)}) collective-permute-start(f32[2,96,128]{2,1,0:T(8,128)S(1)} %pad_maximum_fusion.5), channel_id=1, source_target_pairs={{0,6},{1,7},{2,4},{3,5},{4,2},{5,3},{6,0},{7,1},{8,14},{9,15},{10,... | collective-permute-start | bytes 294920 | tf_op jit(solution)/shard_map/ppermute | solution.py:28
  43.6 14.5 %copy-start.2 = (f32[104,128]{1,0:T(8,128)}, f32[104,128]{1,0:T(8,128)S(1)}, u32[]{:S(2)}) copy-start(f32[104,128]{1,0:T(8,128)S(1)} %collective-permute-done.5) | copy-start | bytes 159748
  44.3 17.3 %collective-permute-start.6 = (f32[2,104,128]{2,1,0:T(8,128)}, f32[2,104,128]{2,1,0:T(8,128)}, u32[]{:S(2)}, u32[]{:S(2)}) collective-permute-start(f32[2,104,128]{2,1,0:T(8,128)} %pad_maximum_fusion.4), channel_id=1, source_target_pairs={{0,64},{1,65},{2,66},{3,67},{4,68},{5,69},{6,70},{7,71},{8,72},{9,... | collective-permute-start | bytes 319496 | tf_op jit(solution)/shard_map/ppermute | solution.py:28
  50.9 12.1 %collective-permute-start.7 = (f32[2,104,128]{2,1,0:T(8,128)}, f32[2,104,128]{2,1,0:T(8,128)}, u32[]{:S(2)}, u32[]{:S(2)}) collective-permute-start(f32[2,104,128]{2,1,0:T(8,128)} %pad_maximum_fusion.4), channel_id=1, source_target_pairs={{0,128},{1,129},{2,130},{3,131},{4,132},{5,133},{6,134},{7,135},{8... | collective-permute-start | bytes 319496 | tf_op jit(solution)/shard_map/ppermute | solution.py:28
  54.2 10.2 %collective-permute-start.8 = (f32[2,104,128]{2,1,0:T(8,128)}, f32[2,104,128]{2,1,0:T(8,128)}, u32[]{:S(2)}, u32[]{:S(2)}) collective-permute-start(f32[2,104,128]{2,1,0:T(8,128)} %pad_maximum_fusion.4), channel_id=1, source_target_pairs={{0,192},{1,193},{2,194},{3,195},{4,196},{5,197},{6,198},{7,199},{8... | collective-permute-start | bytes 319496 | tf_op jit(solution)/shard_map/ppermute | solution.py:28
  76.6 1.0 copy-start.1
  78.5 7.3 %collective-permute-start.9 = (f32[264,512]{1,0:T(8,128)}, f32[264,512]{1,0:T(8,128)}, u32[]{:S(2)}, u32[]{:S(2)}) collective-permute-start(f32[264,512]{1,0:T(8,128)} %maximum_maximum_fusion), channel_id=1, source_target_pairs={{0,8},{1,9},{2,10},{3,11},{4,12},{5,13},{6,14},{7,15},{8,0},{9,1},... | collective-permute-start | bytes 1622024 | tf_op jit(solution)/shard_map/ppermute | solution.py:28
  88.8 9.4 %collective-permute-start.10 = (f32[72,512]{1,0:T(8,128)S(1)}, f32[72,512]{1,0:T(8,128)S(1)}, u32[]{:S(2)}, u32[]{:S(2)}) collective-permute-start(f32[72,512]{1,0:T(8,128)S(1)} %get-tuple-element.9), channel_id=1, source_target_pairs={{0,32},{1,33},{2,34},{3,35},{4,36},{5,37},{6,38},{7,39},{8,40},{9,... | collective-permute-start | bytes 442376 | tf_op jit(solution)/shard_map/ppermute | solution.py:28
  93.4 6.8 %collective-permute-start.11 = (f32[72,512]{1,0:T(8,128)S(1)}, f32[72,512]{1,0:T(8,128)S(1)}, u32[]{:S(2)}, u32[]{:S(2)}) collective-permute-start(f32[72,512]{1,0:T(8,128)S(1)} %get-tuple-element.10), channel_id=1, source_target_pairs={{0,16},{1,17},{2,18},{3,19},{4,20},{5,21},{6,22},{7,23},{8,24},{9,... | collective-permute-start | bytes 442376 | tf_op jit(solution)/shard_map/ppermute | solution.py:28
  95.7 7.5 %collective-permute-start.12 = (f32[72,512]{1,0:T(8,128)S(1)}, f32[72,512]{1,0:T(8,128)S(1)}, u32[]{:S(2)}, u32[]{:S(2)}) collective-permute-start(f32[72,512]{1,0:T(8,128)S(1)} %get-tuple-element.8), channel_id=1, source_target_pairs={{0,48},{1,49},{2,50},{3,51},{4,52},{5,53},{6,54},{7,55},{8,56},{9,... | collective-permute-start | bytes 442376 | tf_op jit(solution)/shard_map/ppermute | solution.py:28

commit v2 on v1

v2 whole, which is shorter than its diff:
```python
import functools
import math

import jax
import jax.numpy as jnp
from jax import lax
from jax.experimental import pallas as pl
from jax.experimental.pallas import tpu as pltpu
from jax.sharding import PartitionSpec as P

AXES = ("env", "sp")
ZL, X, C, Y, ZH = 8, 4, 2, 4, 2
KINDS = 4
LANES = 128
VMEM = pl.BlockSpec(memory_space=pltpu.VMEM)
SMEM = pl.BlockSpec(memory_space=pltpu.SMEM)
F32, BF16 = jnp.float32, jnp.bfloat16


def pairs(move):
    out = []
    for zl in range(ZL):
        for x in range(X):
            for c in range(C):
                for y in range(Y):
                    for zh in range(ZH):
                        a, b, d, e, f = move(zl, x, c, y, zh)
                        here = (((zl * X + x) * C + c) * Y + y) * ZH + zh
                        there = (((a * X + b) * C + d) * Y + e) * ZH + f
                        out.append((here, there))
    return out


def send(value, move):
    return lax.ppermute(value, AXES, pairs(move))


def over_z(m):
    return lambda zl, x, c, y, zh: (zl ^ m, x, c, y, zh)


def over_y(m):
    return lambda zl, x, c, y, zh: (zl, x, c, y ^ m, zh)


def over_x(m):
    return lambda zl, x, c, y, zh: (zl, x ^ m, c, y, zh)


def over_core(zl, x, c, y, zh):
    return (zl, x, 1 - c, y, zh)


def turned(flip):
    return lambda zl, x, c, y, zh: (y * ZH + zh, x, c, zl // ZH, (zl % ZH) ^ flip)


def halves(value):
    high = value.astype(BF16)
    return high, (value - high.astype(F32)).astype(BF16)


def weigh(steps, total, depth, desc, kinds, labels, energies, points, point_kinds, wire, acc, onehot, counts):
    step = pl.program_id(0)
    chunk, structs = desc.shape[0], energies.shape[1]

    @pl.when(step == 0)
    def _():
        own = jnp.concatenate([kinds[j : j + 1] for j in range(kinds.shape[0])], axis=1)
        code = own * structs + labels[...]
        row = lax.broadcasted_iota(jnp.int32, (KINDS * structs, code.shape[1]), 0)
        hits = (row == code).astype(F32)
        onehot[...] = hits.astype(BF16)
        counts[...] = jnp.broadcast_to(jnp.sum(hits, axis=1, keepdims=True), counts.shape)

    dots = lax.dot_general(desc[...], points[...], (((1,), (1,)), ((), ())), preferred_element_type=F32)
    squares = dots * dots
    high, low = halves(squares * squares)
    chosen = onehot[:, pl.ds(pl.multiple_of(step * chunk, chunk), chunk)]
    summed = jnp.dot(chosen, high, preferred_element_type=F32) + jnp.dot(
        chosen, low, preferred_element_type=F32
    )

    @pl.when(step == 0)
    def _():
        acc[...] = summed

    @pl.when(step > 0)
    def _():
        acc[...] += summed

    @pl.when(step == steps - 1)
    def _():
        count = sum(counts[k * structs : (k + 1) * structs, :1] for k in range(KINDS))
        factor = (1.0 / math.sqrt(total)) / count * (1.0 / float(depth) ** 2)
        mine = point_kinds[...]
        weighted = jnp.zeros((structs, acc.shape[1]), F32)
        for k in range(KINDS):
            weighted = weighted + jnp.where(mine == k, acc[k * structs : (k + 1) * structs], 0.0)
        weighted = weighted * factor
        r = lax.broadcasted_iota(jnp.int32, (structs, structs), 0)
        q = lax.broadcasted_iota(jnp.int32, (structs, structs), 1)
        column = jnp.sum(jnp.where(r == q, energies[...], 0.0), axis=1, keepdims=True)
        rhs = jnp.sum(weighted * column, axis=0, keepdims=True)
        for j in range(acc.shape[1] // LANES):
            wire[j * structs : (j + 1) * structs] = weighted[:, j * LANES : (j + 1) * LANES]
        spare = jnp.zeros((4, LANES), F32)
        wire[4 * structs :] = jnp.concatenate(
            [rhs[:, j * LANES : (j + 1) * LANES] for j in range(4)] + [spare]
        )


def weigh_call(descriptors, kinds, labels, energies, points, point_kinds, total):
    envs, depth = descriptors.shape
    cols, structs = points.shape[0], energies.shape[1]
    chunk = envs // 2
    steps = envs // chunk
    whole = lambda i: (0, 0)
    return pl.pallas_call(
        functools.partial(weigh, steps, total, depth),
        grid=(steps,),
        in_specs=[
            pl.BlockSpec((chunk, depth), lambda i: (i, 0)),
            pl.BlockSpec(kinds.shape, whole),
            pl.BlockSpec((1, envs), whole),
            pl.BlockSpec((1, structs), whole),
            pl.BlockSpec((cols, depth), whole),
            pl.BlockSpec((1, cols), whole),
        ],
        out_specs=pl.BlockSpec((4 * structs + 8, LANES), whole),
        out_shape=jax.ShapeDtypeStruct((4 * structs + 8, LANES), F32),
        scratch_shapes=[
            pltpu.VMEM((KINDS * structs, cols), F32),
            pltpu.VMEM((KINDS * structs, envs), BF16),
            pltpu.VMEM((KINDS * structs, LANES), F32),
        ],
        compiler_params=pltpu.CompilerParams(vmem_limit_bytes=56 << 20),
        cost_estimate=pl.CostEstimate(
            flops=2 * envs * depth * cols, bytes_accessed=2 * depth * (envs + cols), transcendentals=0
        ),
        name="weigh",
    )(descriptors, kinds, labels, energies, points, point_kinds)


def simple(kernel, shapes, inputs, scratch=(), flops=0, name=None, limit=8):
    moved = sum(4 * math.prod(a.shape) for a in inputs) + sum(4 * math.prod(s) for s in shapes)
    return pl.pallas_call(
        kernel,
        out_shape=[jax.ShapeDtypeStruct(s, F32) for s in shapes],
        in_specs=[SMEM if a.dtype == jnp.int32 else VMEM for a in inputs],
        out_specs=[VMEM] * len(shapes),
        scratch_shapes=list(scratch),
        compiler_params=pltpu.CompilerParams(vmem_limit_bytes=limit << 20),
        cost_estimate=pl.CostEstimate(flops=flops, bytes_accessed=moved, transcendentals=0),
        name=name,
    )(*inputs)


def pack(first, second, out):
    if len(first.shape) == 2:
        out[0], out[1] = first[...], second[...]
    else:
        half = first.shape[0]
        out[:half], out[half:] = first[...], second[...]


def join(first, second, name):
    lead = 2 if first.ndim == 2 else 2 * first.shape[0]
    (out,) = simple(pack, [(lead,) + first.shape[-2:]], [first, second], name=name)
    return out


A_ORDER = (0, 4, 2, 6, 1, 5, 3, 7)


def tile(structs, owned, where, a0, a1, b0, b1, give, keep, a_all, b_all, b_rows, product):
    cols = a_all.shape[1]
    for j in range(4):
        b_rows[j], b_rows[4 + j] = b0[j], b1[j]
    swap, core = where[0], where[1]
    rhs = jnp.zeros((8, LANES), F32)
    for p, m in enumerate(A_ORDER):
        a = (a0 if p < 4 else a1).at[p % 4]
        rhs = rhs + a[4 * structs :]
        b = b_rows.at[jnp.bitwise_xor(swap, m)]
        for j in range(cols // LANES):
            block = (pl.ds(p * structs, structs), pl.ds(j * LANES, LANES))
            a_all[block] = a[j * structs : (j + 1) * structs]
            b_all[block] = b[j * structs : (j + 1) * structs]
    a_high, a_low = halves(a_all[...])
    b_high, b_low = halves(b_all[...].T)
    product[...] = jnp.dot(b_high, a_high, preferred_element_type=F32) + (
        jnp.dot(b_high, a_low, preferred_element_type=F32)
        + jnp.dot(b_low, a_high, preferred_element_type=F32)
    )
    for x in range(X):
        here = pl.multiple_of(x * C * owned + core * owned, owned)
        there = pl.multiple_of(x * C * owned + (1 - core) * owned, owned)
        keep[x * owned : (x + 1) * owned] = product[pl.ds(here, owned)]
        give[x * owned : (x + 1) * owned] = product[pl.ds(there, owned)]
    row = lax.broadcasted_iota(jnp.int32, (8, cols), 0)
    line = jnp.concatenate([rhs[j : j + 1] for j in range(4)], axis=1)
    line = jnp.where(row == 0, line, 0.0)
    keep[X * owned :] = line
    give[X * owned :] = line


def scatter(owned, where, mine, got, stay, to1, to2, to3, total):
    total[...] = mine[...] + got[...]
    line = total[X * owned :]
    for m, out in enumerate((stay, to1, to2, to3)):
        start = pl.multiple_of(jnp.bitwise_xor(where[2], m) * owned, owned)
        out[:owned] = total[pl.ds(start, owned)]
        out[owned:] = line


def last(owned, stay, f1, f2, f3, gram, rhs):
    total = (stay[...] + f1[...]) + (f2[...] + f3[...])
    gram[...] = total[:owned]
    rhs[...] = total[owned : owned + 1]


def local(descriptors, env_species, structure, energies, sparse_points, sparse_species):
    structs, cols = energies.shape[0], sparse_points.shape[0]
    owned = cols // (X * C)
    env, sp = lax.axis_index("env"), lax.axis_index("sp")
    where = jnp.stack([(env // (X * C)) ^ sp, env % C, env // C % X]).astype(jnp.int32)

    wire = weigh_call(
        descriptors,
        env_species.reshape(-1, LANES),
        structure,
        energies[None],
        sparse_points,
        sparse_species[None],
        structs * ZL * X * C,
    )
    rows = 4 * structs
    cut = wire[:rows]
    far = send(wire, over_z(4))
    t0 = send(cut, turned(0))
    t1 = send(cut, turned(1))
    a_two = join(wire, far, "pack_a_two")
    a_got = send(a_two, over_z(2))
    b_two = join(t0, t1, "pack_b_two")
    b_got = send(b_two, over_y(1))
    a_four = join(a_two, a_got, "pack_a_four")
    a_more = send(a_four, over_z(1))
    b_four = join(b_two, b_got, "pack_b_four")
    b_more = send(b_four, over_y(2))
    half = X * owned
    give, keep = simple(
        functools.partial(tile, structs, owned),
        [(half + 8, cols)] * 2,
        [where, a_four, a_more, b_four, b_more],
        scratch=[
            pltpu.VMEM((8 * structs, cols), F32),
            pltpu.VMEM((8 * structs, cols), F32),
            pltpu.VMEM((8, rows, LANES), F32),
            pltpu.VMEM((cols, cols), F32),
        ],
        flops=6 * cols * cols * 8 * structs,
        name="tile",
        limit=16,
    )
    got = send(give, over_core)
    parts = simple(
        functools.partial(scatter, owned),
        [(owned + 8, cols)] * 4,
        [where, keep, got],
        scratch=[pltpu.VMEM((half + 8, cols), F32)],
        name="scatter",
    )
    came = [send(parts[m], over_x(m)) for m in (2, 1, 3)]
    gram, rhs = simple(
        functools.partial(last, owned), [(owned, cols), (1, cols)], [parts[0], *came], name="last"
    )
    return gram.T, rhs[0]


def solution(mesh):
    in_specs = (P("env", None), P("env"), P("env", None), P("env"), P("sp", None), P("sp"))
    out_specs = (P("sp", "env"), P("sp"))
    return jax.shard_map(local, mesh=mesh, in_specs=in_specs, out_specs=out_specs, check_vma=False)
```

time: 106 us -> 76.1 us (0.72)
  the two profiles are of different devices: /device:TPU:1 before, /device:TPU:24 now
where the time goes in v2:
time: 76.1 us; the launch traced here: 75.6 us
  starting transfers between devices  46.2 us (61%)
  waiting for transfers between devices  18.9 us (25%)
  Pallas kernels  8.03 us (11%)
  local copies, waits for them, and re-layouts  1.62 us (2%)
  between operations  0.83 us (1%)
    ppermute x11, starting transfers between devices, send(): return lax.ppermute(value, AXES, pairs(move))  46.2 us
    ppermute x11, waiting for transfers between devices, send(): return lax.ppermute(value, AXES, pairs(move))  18.9 us
    pallas_call x1, Pallas kernels, weigh_call(): pl.pallas_call(functools.partial(weigh, steps, total, depth), grid=(steps...  5.41 us
    pallas_call x7, Pallas kernels, simple(): pl.pallas_call(kernel, out_shape=[jax.ShapeDtypeStruct(s, F32) for s in s...  2.62 us
  transfers between devices with their start and end apart: 11, of which 7 were waited for; matrix products, arithmetic and copies ran while one was open for 1% of the time, Pallas kernels for 0%

profile of v2, /device:TPU:24, one launch (start us, length us, event | category | flops | bytes accessed | tf_op | source)
XLA Modules:
  0.0 75.6 jit_solution(6681500668054009770)
XLA Ops:
  0.6 5.4 %weigh.1.first = f32[104,128]{1,0:T(8,128)} custom-call(bf16[1536,1024]{1,0:T(8,128)(2,1)} %desc.1, s32[12,128]{1,0:T(8,128)} %bitcast.9, s32[1,1536]{1,0:T(1,128)} %labels.1, f32[1,24]{1,0:T(1,128)} %bitcast.12, bf16[512,1024]{1,0:T(8,128)(2,1)} %points.1, s32[1,512]{1,0:T(1,128)} %bitcast.10), custom_call_target="tpu_custom_call" | custom-call | flops 1610612736 | bytes 4194304 | tf_op jit(solution)/shard_map/weigh/pallas_call | solution.py:119
  6.0 9.1 %collective-permute-start = (f32[104,128]{1,0:T(8,128)}, f32[104,128]{1,0:T(8,128)S(1)}, u32[]{:S(2)}, u32[]{:S(2)}) collective-permute-start(f32[104,128]{1,0:T(8,128)} %weigh.1.first), channel_id=1, source_target_pairs={{0,256},{1,257},{2,258},{3,259},{4,260},{5,261},{6,262},{7,263},{8... | collective-permute-start | bytes 159752 | tf_op jit(solution)/shard_map/ppermute | solution.py:35
  15.1 0.8 %slice.4 = f32[96,128]{1,0:T(8,128)S(1)} slice(f32[104,128]{1,0:T(8,128)} %weigh.1.first), slice={[0:96], [0:128]} | slice | bytes 98304 | tf_op jit(solution)/shard_map/slice | solution.py:239
  15.9 7.9 %collective-permute-start.4 = (f32[96,128]{1,0:T(8,128)S(1)}, f32[96,128]{1,0:T(8,128)S(1)}, u32[]{:S(2)}, u32[]{:S(2)}) collective-permute-start(f32[96,128]{1,0:T(8,128)S(1)} %slice.4), channel_id=1, source_target_pairs={{0,1},{1,65},{2,129},{3,193},{4,257},{5,321},{6,385},{7,449},{8,9}... | collective-permute-start | bytes 147464 | tf_op jit(solution)/shard_map/ppermute | solution.py:35
  23.8 7.6 %collective-permute-start.3 = (f32[96,128]{1,0:T(8,128)S(1)}, f32[96,128]{1,0:T(8,128)S(1)}, u32[]{:S(2)}, u32[]{:S(2)}) collective-permute-start(f32[96,128]{1,0:T(8,128)S(1)} %slice.4), channel_id=1, source_target_pairs={{0,0},{1,64},{2,128},{3,192},{4,256},{5,320},{6,384},{7,448},{8,8}... | collective-permute-start | bytes 147464 | tf_op jit(solution)/shard_map/ppermute | solution.py:35
  31.5 0.0 collective-permute-done.second
  31.5 0.0 copy-start
  31.5 0.8 %copy-done = f32[104,128]{1,0:T(8,128)S(1)} copy-done((f32[104,128]{1,0:T(8,128)S(1)}, f32[104,128]{1,0:T(8,128)}, u32[]{:S(2)}) %copy-start) | copy-done | bytes 53272
  32.3 3.7 %collective-permute-start.1 = (f32[2,104,128]{2,1,0:T(8,128)S(1)}, f32[2,104,128]{2,1,0:T(8,128)S(1)}, u32[]{:S(2)}, u32[]{:S(2)}) collective-permute-start(f32[2,104,128]{2,1,0:T(8,128)S(1)} %pack_a_two.1.first), channel_id=1, source_target_pairs={{0,128},{1,129},{2,130},{3,131},{4,132},{5,133},{6,134},{7,135},{8... | collective-permute-start | bytes 319496 | tf_op jit(solution)/shard_map/ppermute | solution.py:35
  36.0 0.0 collective-permute-done.4.second
  36.0 1.7 %collective-permute-done.3.first = f32[96,128]{1,0:T(8,128)S(1)} collective-permute-done((f32[96,128]{1,0:T(8,128)S(1)}, f32[96,128]{1,0:T(8,128)S(1)}, u32[]{:S(2)}, u32[]{:S(2)}) %collective-permute-start.3) | collective-permute-done | bytes 49184 | tf_op jit(solution)/shard_map/ppermute | solution.py:35
  37.7 2.2 %collective-permute-start.5 = (f32[2,96,128]{2,1,0:T(8,128)S(1)}, f32[2,96,128]{2,1,0:T(8,128)S(1)}, u32[]{:S(2)}, u32[]{:S(2)}) collective-permute-start(f32[2,96,128]{2,1,0:T(8,128)S(1)} %pack_b_two.1.first), channel_id=1, source_target_pairs={{0,2},{1,3},{2,0},{3,1},{4,6},{5,7},{6,4},{7,5},{8,10},{9,11},{10,... | collective-permute-start | bytes 294920 | tf_op jit(solution)/shard_map/ppermute | solution.py:35
  39.9 1.3 %collective-permute-done.1.second = f32[2,104,128]{2,1,0:T(8,128)S(1)} collective-permute-done((f32[2,104,128]{2,1,0:T(8,128)S(1)}, f32[2,104,128]{2,1,0:T(8,128)S(1)}, u32[]{:S(2)}, u32[]{:S(2)}) %collective-permute-start.1) | collective-permute-done | bytes 106528 | tf_op jit(solution)/shard_map/ppermute | solution.py:35
  41.3 1.9 %collective-permute-start.2 = (f32[4,104,128]{2,1,0:T(8,128)S(1)}, f32[4,104,128]{2,1,0:T(8,128)S(1)}, u32[]{:S(2)}, u32[]{:S(2)}) collective-permute-start(f32[4,104,128]{2,1,0:T(8,128)S(1)} %pack_a_four.1.a0), channel_id=1, source_target_pairs={{0,64},{1,65},{2,66},{3,67},{4,68},{5,69},{6,70},{7,71},{8,72},{9,... | collective-permute-start | bytes 638984 | tf_op jit(solution)/shard_map/ppermute | solution.py:35
  43.2 1.0 %collective-permute-done.5.second = f32[2,96,128]{2,1,0:T(8,128)S(1)} collective-permute-done((f32[2,96,128]{2,1,0:T(8,128)S(1)}, f32[2,96,128]{2,1,0:T(8,128)S(1)}, u32[]{:S(2)}, u32[]{:S(2)}) %collective-permute-start.5) | collective-permute-done | bytes 98336 | tf_op jit(solution)/shard_map/ppermute | solution.py:35
  44.2 1.9 %collective-permute-start.6 = (f32[4,96,128]{2,1,0:T(8,128)S(1)}, f32[4,96,128]{2,1,0:T(8,128)S(1)}, u32[]{:S(2)}, u32[]{:S(2)}) collective-permute-start(f32[4,96,128]{2,1,0:T(8,128)S(1)} %pack_b_four.1.b0), channel_id=1, source_target_pairs={{0,4},{1,5},{2,6},{3,7},{4,0},{5,1},{6,2},{7,3},{8,12},{9,13},{10,... | collective-permute-start | bytes 589832 | tf_op jit(solution)/shard_map/ppermute | solution.py:35
  46.2 0.1 pad_add_fusion.where
  46.3 7.0 %collective-permute-done.6.b1 = f32[4,96,128]{2,1,0:T(8,128)S(1)} collective-permute-done((f32[4,96,128]{2,1,0:T(8,128)S(1)}, f32[4,96,128]{2,1,0:T(8,128)S(1)}, u32[]{:S(2)}, u32[]{:S(2)}) %collective-permute-start.6) | collective-permute-done | bytes 196640 | tf_op jit(solution)/shard_map/ppermute | solution.py:35
  53.3 0.0 collective-permute-done.2.a1
  53.3 1.3 %tile.1 = (f32[264,512]{1,0:T(8,128)S(1)}, f32[264,512]{1,0:T(8,128)S(1)}) custom-call(s32[3]{0:T(128)S(1)} %pad_add_fusion.where, f32[4,104,128]{2,1,0:T(8,128)S(1)} %pack_a_four.1.a0, f32[4,104,128]{2,1,0:T(8,128)S(1)} %collective-permute-done.2.a1, f32[4,96,128]{2,1,0:T(8,128)S(1)} %pack_b_four.1.b0, f32[4,96,128]{2,1,0:T(8,128)S(1)} %collective-permute-done.6.b1), custom_call_target="tpu_custom_call" | custom-call | flops 301989888 | bytes 1900556 | tf_op jit(solution)/shard_map/tile/pallas_call | solution.py:147
  54.6 1.9 %collective-permute-start.7 = (f32[264,512]{1,0:T(8,128)S(1)}, f32[264,512]{1,0:T(8,128)S(1)}, u32[]{:S(2)}, u32[]{:S(2)}) collective-permute-start(f32[264,512]{1,0:T(8,128)S(1)} %get-tuple-element.11), channel_id=1, source_target_pairs={{0,8},{1,9},{2,10},{3,11},{4,12},{5,13},{6,14},{7,15},{8,0},{9,1},... | collective-permute-start | bytes 1622024 | tf_op jit(solution)/shard_map/ppermute | solution.py:35
  56.5 1.9 %collective-permute-done.7.got = f32[264,512]{1,0:T(8,128)S(1)} collective-permute-done((f32[264,512]{1,0:T(8,128)S(1)}, f32[264,512]{1,0:T(8,128)S(1)}, u32[]{:S(2)}, u32[]{:S(2)}) %collective-permute-start.7) | collective-permute-done | bytes 540704 | tf_op jit(solution)/shard_map/ppermute | solution.py:35
  58.4 0.6 scatter.1
  59.0 4.9 %collective-permute-start.8 = (f32[72,512]{1,0:T(8,128)S(1)}, f32[72,512]{1,0:T(8,128)S(1)}, u32[]{:S(2)}, u32[]{:S(2)}) collective-permute-start(f32[72,512]{1,0:T(8,128)S(1)} %get-tuple-element.13), channel_id=1, source_target_pairs={{0,32},{1,33},{2,34},{3,35},{4,36},{5,37},{6,38},{7,39},{8,40},{9,... | collective-permute-start | bytes 442376 | tf_op jit(solution)/shard_map/ppermute | solution.py:35
  64.0 2.5 %collective-permute-start.9 = (f32[72,512]{1,0:T(8,128)S(1)}, f32[72,512]{1,0:T(8,128)S(1)}, u32[]{:S(2)}, u32[]{:S(2)}) collective-permute-start(f32[72,512]{1,0:T(8,128)S(1)} %get-tuple-element.14), channel_id=1, source_target_pairs={{0,16},{1,17},{2,18},{3,19},{4,20},{5,21},{6,22},{7,23},{8,24},{9,... | collective-permute-start | bytes 442376 | tf_op jit(solution)/shard_map/ppermute | solution.py:35
  66.5 2.5 %collective-permute-start.10 = (f32[72,512]{1,0:T(8,128)S(1)}, f32[72,512]{1,0:T(8,128)S(1)}, u32[]{:S(2)}, u32[]{:S(2)}) collective-permute-start(f32[72,512]{1,0:T(8,128)S(1)} %get-tuple-element.15), channel_id=1, source_target_pairs={{0,48},{1,49},{2,50},{3,51},{4,52},{5,53},{6,54},{7,55},{8,56},{9,... | collective-permute-start | bytes 442376 | tf_op jit(solution)/shard_map/ppermute | solution.py:35
  69.0 0.0 collective-permute-done.8.f1
  69.0 2.6 %collective-permute-done.9.f2 = f32[72,512]{1,0:T(8,128)S(1)} collective-permute-done((f32[72,512]{1,0:T(8,128)S(1)}, f32[72,512]{1,0:T(8,128)S(1)}, u32[]{:S(2)}, u32[]{:S(2)}) %collective-permute-start.9) | collective-permute-done | bytes 147488 | tf_op jit(solution)/shard_map/ppermute | solution.py:35
  71.6 3.3 %collective-permute-done.10.f3 = f32[72,512]{1,0:T(8,128)S(1)} collective-permute-done((f32[72,512]{1,0:T(8,128)S(1)}, f32[72,512]{1,0:T(8,128)S(1)}, u32[]{:S(2)}, u32[]{:S(2)}) %collective-permute-start.10) | collective-permute-done | bytes 147488 | tf_op jit(solution)/shard_map/ppermute | solution.py:35
  74.9 0.7 last.1
  (4 shorter events, 0.0 us)
Async XLA Ops:
  6.0 25.4 %collective-permute-start = (f32[104,128]{1,0:T(8,128)}, f32[104,128]{1,0:T(8,128)S(1)}, u32[]{:S(2)}, u32[]{:S(2)}) collective-permute-start(f32[104,128]{1,0:T(8,128)} %weigh.1.first), channel_id=1, source_target_pairs={{0,256},{1,257},{2,258},{3,259},{4,260},{5,261},{6,262},{7,263},{8... | collective-permute-start | bytes 159752 | tf_op jit(solution)/shard_map/ppermute | solution.py:35
  15.9 20.0 %collective-permute-start.4 = (f32[96,128]{1,0:T(8,128)S(1)}, f32[96,128]{1,0:T(8,128)S(1)}, u32[]{:S(2)}, u32[]{:S(2)}) collective-permute-start(f32[96,128]{1,0:T(8,128)S(1)} %slice.4), channel_id=1, source_target_pairs={{0,1},{1,65},{2,129},{3,193},{4,257},{5,321},{6,385},{7,449},{8,9}... | collective-permute-start | bytes 147464 | tf_op jit(solution)/shard_map/ppermute | solution.py:35
  23.8 13.9 %collective-permute-start.3 = (f32[96,128]{1,0:T(8,128)S(1)}, f32[96,128]{1,0:T(8,128)S(1)}, u32[]{:S(2)}, u32[]{:S(2)}) collective-permute-start(f32[96,128]{1,0:T(8,128)S(1)} %slice.4), channel_id=1, source_target_pairs={{0,0},{1,64},{2,128},{3,192},{4,256},{5,320},{6,384},{7,448},{8,8}... | collective-permute-start | bytes 147464 | tf_op jit(solution)/shard_map/ppermute | solution.py:35
  31.5 0.8 %copy-start = (f32[104,128]{1,0:T(8,128)S(1)}, f32[104,128]{1,0:T(8,128)}, u32[]{:S(2)}) copy-start(f32[104,128]{1,0:T(8,128)} %weigh.1.first) | copy-start | bytes 159748
  32.3 8.9 %collective-permute-start.1 = (f32[2,104,128]{2,1,0:T(8,128)S(1)}, f32[2,104,128]{2,1,0:T(8,128)S(1)}, u32[]{:S(2)}, u32[]{:S(2)}) collective-permute-start(f32[2,104,128]{2,1,0:T(8,128)S(1)} %pack_a_two.1.first), channel_id=1, source_target_pairs={{0,128},{1,129},{2,130},{3,131},{4,132},{5,133},{6,134},{7,135},{8... | collective-permute-start | bytes 319496 | tf_op jit(solution)/shard_map/ppermute | solution.py:35
  37.7 6.5 %collective-permute-start.5 = (f32[2,96,128]{2,1,0:T(8,128)S(1)}, f32[2,96,128]{2,1,0:T(8,128)S(1)}, u32[]{:S(2)}, u32[]{:S(2)}) collective-permute-start(f32[2,96,128]{2,1,0:T(8,128)S(1)} %pack_b_two.1.first), channel_id=1, source_target_pairs={{0,2},{1,3},{2,0},{3,1},{4,6},{5,7},{6,4},{7,5},{8,10},{9,11},{10,... | collective-permute-start | bytes 294920 | tf_op jit(solution)/shard_map/ppermute | solution.py:35
  41.3 12.0 %collective-permute-start.2 = (f32[4,104,128]{2,1,0:T(8,128)S(1)}, f32[4,104,128]{2,1,0:T(8,128)S(1)}, u32[]{:S(2)}, u32[]{:S(2)}) collective-permute-start(f32[4,104,128]{2,1,0:T(8,128)S(1)} %pack_a_four.1.a0), channel_id=1, source_target_pairs={{0,64},{1,65},{2,66},{3,67},{4,68},{5,69},{6,70},{7,71},{8,72},{9,... | collective-permute-start | bytes 638984 | tf_op jit(solution)/shard_map/ppermute | solution.py:35
  44.2 9.1 %collective-permute-start.6 = (f32[4,96,128]{2,1,0:T(8,128)S(1)}, f32[4,96,128]{2,1,0:T(8,128)S(1)}, u32[]{:S(2)}, u32[]{:S(2)}) collective-permute-start(f32[4,96,128]{2,1,0:T(8,128)S(1)} %pack_b_four.1.b0), channel_id=1, source_target_pairs={{0,4},{1,5},{2,6},{3,7},{4,0},{5,1},{6,2},{7,3},{8,12},{9,13},{10,... | collective-permute-start | bytes 589832 | tf_op jit(solution)/shard_map/ppermute | solution.py:35
  54.6 3.8 %collective-permute-start.7 = (f32[264,512]{1,0:T(8,128)S(1)}, f32[264,512]{1,0:T(8,128)S(1)}, u32[]{:S(2)}, u32[]{:S(2)}) collective-permute-start(f32[264,512]{1,0:T(8,128)S(1)} %get-tuple-element.11), channel_id=1, source_target_pairs={{0,8},{1,9},{2,10},{3,11},{4,12},{5,13},{6,14},{7,15},{8,0},{9,1},... | collective-permute-start | bytes 1622024 | tf_op jit(solution)/shard_map/ppermute | solution.py:35
  59.0 9.9 %collective-permute-start.8 = (f32[72,512]{1,0:T(8,128)S(1)}, f32[72,512]{1,0:T(8,128)S(1)}, u32[]{:S(2)}, u32[]{:S(2)}) collective-permute-start(f32[72,512]{1,0:T(8,128)S(1)} %get-tuple-element.13), channel_id=1, source_target_pairs={{0,32},{1,33},{2,34},{3,35},{4,36},{5,37},{6,38},{7,39},{8,40},{9,... | collective-permute-start | bytes 442376 | tf_op jit(solution)/shard_map/ppermute | solution.py:35
  64.0 7.6 %collective-permute-start.9 = (f32[72,512]{1,0:T(8,128)S(1)}, f32[72,512]{1,0:T(8,128)S(1)}, u32[]{:S(2)}, u32[]{:S(2)}) collective-permute-start(f32[72,512]{1,0:T(8,128)S(1)} %get-tuple-element.14), channel_id=1, source_target_pairs={{0,16},{1,17},{2,18},{3,19},{4,20},{5,21},{6,22},{7,23},{8,24},{9,... | collective-permute-start | bytes 442376 | tf_op jit(solution)/shard_map/ppermute | solution.py:35
  66.5 8.4 %collective-permute-start.10 = (f32[72,512]{1,0:T(8,128)S(1)}, f32[72,512]{1,0:T(8,128)S(1)}, u32[]{:S(2)}, u32[]{:S(2)}) collective-permute-start(f32[72,512]{1,0:T(8,128)S(1)} %get-tuple-element.15), channel_id=1, source_target_pairs={{0,48},{1,49},{2,50},{3,51},{4,52},{5,53},{6,54},{7,55},{8,56},{9,... | collective-permute-start | bytes 442376 | tf_op jit(solution)/shard_map/ppermute | solution.py:35

commit v3 on v2

v3 whole, which is shorter than its diff:
```python
import functools
import math

import jax
import jax.numpy as jnp
from jax import lax
from jax.experimental import pallas as pl
from jax.experimental.pallas import tpu as pltpu
from jax.sharding import PartitionSpec as P

AXES = ("env", "sp")
ZL, X, C, Y, ZH = 8, 4, 2, 4, 2
KINDS = 4
LANES = 128
VMEM = pl.BlockSpec(memory_space=pltpu.VMEM)
SMEM = pl.BlockSpec(memory_space=pltpu.SMEM)
F32, BF16 = jnp.float32, jnp.bfloat16


def pairs(move):
    out = []
    for zl in range(ZL):
        for x in range(X):
            for c in range(C):
                for y in range(Y):
                    for zh in range(ZH):
                        a, b, d, e, f = move(zl, x, c, y, zh)
                        here = (((zl * X + x) * C + c) * Y + y) * ZH + zh
                        there = (((a * X + b) * C + d) * Y + e) * ZH + f
                        out.append((here, there))
    return out


def send(value, move):
    return lax.ppermute(value, AXES, pairs(move))


def over_z(m):
    return lambda zl, x, c, y, zh: (zl ^ m, x, c, y, zh)


def over_y(m):
    return lambda zl, x, c, y, zh: (zl, x, c, y ^ m, zh)


def over_x(m):
    return lambda zl, x, c, y, zh: (zl, x ^ m, c, y, zh)


def over_core(zl, x, c, y, zh):
    return (zl, x, 1 - c, y, zh)


def turned(flip):
    return lambda zl, x, c, y, zh: (y * ZH + zh, x, c, zl // ZH, (zl % ZH) ^ flip)


def halves(value):
    high = value.astype(BF16)
    return high, (value - high.astype(F32)).astype(BF16)


def weigh(chunks, total, desc, kinds, labels, energies, points, point_kinds, wire, cut, *scratch):
    desc_here, points_here, kinds_here, labels_here, energies_here, point_kinds_here, sems = scratch
    (envs, depth), cols, structs = desc.shape, points.shape[0], energies.shape[1]
    firsts = [sum(chunks[:i]) for i in range(len(chunks))]
    small = [
        pltpu.make_async_copy(source, target, sems.at[i])
        for i, (source, target) in enumerate(
            (
                (points, points_here),
                (kinds, kinds_here),
                (labels, labels_here),
                (energies, energies_here),
                (point_kinds, point_kinds_here),
            )
        )
    ]
    large = [
        pltpu.make_async_copy(
            desc.at[pl.ds(first, size)], desc_here.at[pl.ds(first, size)], sems.at[len(small) + i]
        )
        for i, (first, size) in enumerate(zip(firsts, chunks))
    ]
    small[0].start()
    large[0].start()
    for copy in small[1:] + large[1:]:
        copy.start()
    small[1].wait()
    small[2].wait()
    own = jnp.concatenate([kinds_here[j : j + 1] for j in range(kinds.shape[0])], axis=1)
    code = own * structs + labels_here[...]
    row = lax.broadcasted_iota(jnp.int32, (KINDS * structs, envs), 0)
    hits = (row == code).astype(F32)
    counts = jnp.sum(hits, axis=1, keepdims=True)
    onehot = hits.astype(BF16)
    small[0].wait()
    acc = jnp.zeros((KINDS * structs, cols), F32)
    for copy, first, size in zip(large, firsts, chunks):
        copy.wait()
        dots = lax.dot_general(
            desc_here[first : first + size],
            points_here[...],
            (((1,), (1,)), ((), ())),
            preferred_element_type=F32,
        )
        squares = dots * dots
        high, low = halves(squares * squares)
        chosen = onehot[:, first : first + size]
        acc = acc + (
            jnp.dot(chosen, high, preferred_element_type=F32)
            + jnp.dot(chosen, low, preferred_element_type=F32)
        )
    small[3].wait()
    small[4].wait()
    count = sum(counts[k * structs : (k + 1) * structs] for k in range(KINDS))
    factor = (1.0 / math.sqrt(total)) / count * (1.0 / float(depth) ** 2)
    mine = point_kinds_here[...]
    weighted = jnp.zeros((structs, cols), F32)
    for k in range(KINDS):
        weighted = weighted + jnp.where(mine == k, acc[k * structs : (k + 1) * structs], 0.0)
    weighted = weighted * factor
    r = lax.broadcasted_iota(jnp.int32, (structs, structs), 0)
    q = lax.broadcasted_iota(jnp.int32, (structs, structs), 1)
    column = jnp.sum(jnp.where(r == q, energies_here[...], 0.0), axis=1, keepdims=True)
    rhs = jnp.sum(weighted * column, axis=0, keepdims=True)
    for j in range(cols // LANES):
        here = slice(j * structs, (j + 1) * structs)
        wire[here] = cut[here] = weighted[:, j * LANES : (j + 1) * LANES]
    spare = jnp.zeros((4, LANES), F32)
    wire[4 * structs :] = jnp.concatenate(
        [rhs[:, j * LANES : (j + 1) * LANES] for j in range(4)] + [spare]
    )


def weigh_call(descriptors, kinds, labels, energies, points, point_kinds, total):
    envs, depth = descriptors.shape
    cols, structs = points.shape[0], energies.shape[1]
    chunks = (envs // 6, envs // 3, envs // 2)
    inputs = (descriptors, kinds, labels, energies, points, point_kinds)
    held = (descriptors, points, kinds, labels, energies, point_kinds)
    return pl.pallas_call(
        functools.partial(weigh, chunks, total),
        in_specs=[pl.BlockSpec(memory_space=pltpu.HBM)] * len(inputs),
        out_specs=[VMEM, VMEM],
        out_shape=[jax.ShapeDtypeStruct((rows, LANES), F32) for rows in (4 * structs + 8, 4 * structs)],
        scratch_shapes=[pltpu.VMEM(a.shape, a.dtype) for a in held]
        + [pltpu.SemaphoreType.DMA((5 + len(chunks),))],
        compiler_params=pltpu.CompilerParams(vmem_limit_bytes=56 << 20),
        cost_estimate=pl.CostEstimate(
            flops=2 * envs * depth * cols, bytes_accessed=2 * depth * (envs + cols), transcendentals=0
        ),
        name="weigh",
    )(*inputs)


def simple(kernel, shapes, inputs, scratch=(), flops=0, name=None, limit=8):
    moved = sum(4 * math.prod(a.shape) for a in inputs) + sum(4 * math.prod(s) for s in shapes)
    return pl.pallas_call(
        kernel,
        out_shape=[jax.ShapeDtypeStruct(s, F32) for s in shapes],
        in_specs=[SMEM if a.dtype == jnp.int32 else VMEM for a in inputs],
        out_specs=[VMEM] * len(shapes),
        scratch_shapes=list(scratch),
        compiler_params=pltpu.CompilerParams(vmem_limit_bytes=limit << 20),
        cost_estimate=pl.CostEstimate(flops=flops, bytes_accessed=moved, transcendentals=0),
        name=name,
    )(*inputs)


def pack(first, second, out):
    if len(first.shape) == 2:
        out[0], out[1] = first[...], second[...]
    else:
        half = first.shape[0]
        out[:half], out[half:] = first[...], second[...]


def join(first, second, name):
    lead = 2 if first.ndim == 2 else 2 * first.shape[0]
    (out,) = simple(pack, [(lead,) + first.shape[-2:]], [first, second], name=name)
    return out


A_ORDER = (0, 4, 2, 6, 1, 5, 3, 7)


def tile(structs, owned, where, a0, a1, b0, b1, give, keep, a_all, b_all, b_rows, product):
    cols = a_all.shape[1]
    for j in range(4):
        b_rows[j], b_rows[j ^ 6] = b0[j], b1[j]
    swap, core = where[0], where[1]
    rhs = jnp.zeros((8, LANES), F32)
    for p, m in enumerate(A_ORDER):
        a = (a0 if p < 4 else a1).at[p % 4]
        rhs = rhs + a[4 * structs :]
        b = b_rows.at[jnp.bitwise_xor(swap, m)]
        for j in range(cols // LANES):
            block = (pl.ds(p * structs, structs), pl.ds(j * LANES, LANES))
            a_all[block] = a[j * structs : (j + 1) * structs]
            b_all[block] = b[j * structs : (j + 1) * structs]
    a_high, a_low = halves(a_all[...])
    b_high, b_low = halves(b_all[...].T)
    product[...] = jnp.dot(b_high, a_high, preferred_element_type=F32) + (
        jnp.dot(b_high, a_low, preferred_element_type=F32)
        + jnp.dot(b_low, a_high, preferred_element_type=F32)
    )
    line = jnp.concatenate([rhs[:4], jnp.zeros((4, LANES), F32)])
    lanes = cols // LANES
    for half, out in ((core, keep), (1 - core, give)):
        for x in range(X):
            first = pl.multiple_of((x * C + half) * owned, owned)
            for j in range(lanes):
                out[pl.ds((x * lanes + j) * owned, owned)] = product[
                    pl.ds(first, owned), j * LANES : (j + 1) * LANES
                ]
        out[X * lanes * owned :] = line


def scatter(mine, got, out):
    piece = out.shape[1] - 8
    line = mine[X * piece :] + got[X * piece :]
    for x in range(X):
        out[x, :piece] = mine[x * piece : (x + 1) * piece] + got[x * piece : (x + 1) * piece]
        out[x, piece:] = line


def last(owned, came, gram, rhs):
    total = (came[0] + came[1]) + (came[2] + came[3])
    for j in range(gram.shape[1] // LANES):
        gram[:, j * LANES : (j + 1) * LANES] = total[j * owned : (j + 1) * owned]
    tail = total[came.shape[1] - 8 :]
    rhs[...] = jnp.concatenate([tail[j : j + 1] for j in range(4)], axis=1)


def x_groups():
    return [
        [((z * X + x) * C + c) * Y * ZH + s for x in range(X)]
        for z in range(ZL)
        for c in range(C)
        for s in range(Y * ZH)
    ]


def local(descriptors, env_species, structure, energies, sparse_points, sparse_species):
    structs, cols = energies.shape[0], sparse_points.shape[0]
    owned = cols // (X * C)
    env, sp = lax.axis_index("env"), lax.axis_index("sp")
    where = jnp.stack([(env // (X * C)) ^ sp, env % C, env // C % X]).astype(jnp.int32)

    wire, cut = weigh_call(
        descriptors,
        env_species.reshape(-1, LANES),
        structure,
        energies[None],
        sparse_points,
        sparse_species[None],
        structs * ZL * X * C,
    )
    rows = 4 * structs
    far = send(wire, over_z(4))
    t0 = send(cut, turned(0))
    t1 = send(cut, turned(1))
    a_two = join(wire, far, "pack_a_two")
    a_got = send(a_two, over_z(2))
    b_two = join(t0, t1, "pack_b_two")
    b_got = send(b_two, over_y(1))
    a_four = join(a_two, a_got, "pack_a_four")
    a_more = send(a_four, over_z(1))
    b_four = join(b_two, b_got, "pack_b_four")
    b_more = send(b_four, over_y(3))
    piece = owned * (cols // LANES)
    give, keep = simple(
        functools.partial(tile, structs, owned),
        [(X * piece + 8, LANES)] * 2,
        [where, a_four, a_more, b_four, b_more],
        scratch=[
            pltpu.VMEM((8 * structs, cols), F32),
            pltpu.VMEM((8 * structs, cols), F32),
            pltpu.VMEM((8, rows, LANES), F32),
            pltpu.VMEM((cols, cols), F32),
        ],
        flops=6 * cols * cols * 8 * structs,
        name="tile",
        limit=16,
    )
    got = send(give, over_core)
    (parts,) = simple(scatter, [(X, piece + 8, LANES)], [keep, got], name="scatter")
    came = lax.all_to_all(parts, AXES, 0, 0, axis_index_groups=x_groups())
    gram, rhs = simple(
        functools.partial(last, owned), [(owned, cols), (1, cols)], [came], name="last"
    )
    return gram.T, rhs[0]


def solution(mesh):
    in_specs = (P("env", None), P("env"), P("env", None), P("env"), P("sp", None), P("sp"))
    out_specs = (P("sp", "env"), P("sp"))
    return jax.shard_map(local, mesh=mesh, in_specs=in_specs, out_specs=out_specs, check_vma=False)
```

time: 76.1 us -> 72.4 us (0.951)
  blocking collectives: 0 us -> 14 us
  starting transfers between devices: 46.2 us -> 36.3 us
  waiting for transfers between devices: 18.9 us -> 12.8 us
  Pallas kernels: 8.03 us -> 7.12 us
  local copies, waits for them, and re-layouts: 1.62 us -> 0.8 us
    all_to_all x0 -> x1, blocking collectives: none -> 14 us  [local(): came = lax.all_to_all(parts, AXES, 0, 0, axis_index_groups=x_groups())]
    ppermute x11 -> x8, starting transfers between devices: 46.2 us -> 36.3 us  [send(): return lax.ppermute(value, AXES, pairs(move))]
    ppermute x11 -> x8, waiting for transfers between devices: 18.9 us -> 12.8 us  [send(): return lax.ppermute(value, AXES, pairs(move))]
    slice x1 -> x0, local copies, waits for them, and re-layouts: 0.81 us -> none  [local(): cut = wire[:rows]]
  transfers between devices with their start and end apart: 11 -> 8, of which waited for: 7 -> 5; matrix products, arithmetic and copies ran while one was open for 1% -> 0% of each run, Pallas kernels for 0% -> 0%
where the time goes in v3:
time: 72.4 us; the launch traced here: 72 us
  starting transfers between devices  36.3 us (50%)
  blocking collectives  14 us (19%)
  waiting for transfers between devices  12.8 us (18%)
  Pallas kernels  7.12 us (10%)
  local copies, waits for them, and re-layouts  0.8 us (1%)
  between operations  0.8 us (1%)
    ppermute x8, starting transfers between devices, send(): return lax.ppermute(value, AXES, pairs(move))  36.3 us
    all_to_all x1, blocking collectives, local(): came = lax.all_to_all(parts, AXES, 0, 0, axis_index_groups=x_groups())  14 us
    ppermute x8, waiting for transfers between devices, send(): return lax.ppermute(value, AXES, pairs(move))  12.8 us
    pallas_call x1, Pallas kernels, weigh_call(): pl.pallas_call(functools.partial(weigh, chunks, total), in_specs=[pl.Bloc...  5.07 us
    pallas_call x7, Pallas kernels, simple(): pl.pallas_call(kernel, out_shape=[jax.ShapeDtypeStruct(s, F32) for s in s...  2.05 us
  transfers between devices with their start and end apart: 8, of which 5 were waited for; matrix products, arithmetic and copies ran while one was open for 0% of the time, Pallas kernels for 0%

profile of v3, /device:TPU:24, one launch (start us, length us, event | category | flops | bytes accessed | tf_op | source)
XLA Modules:
  0.0 72.0 jit_solution(878066254457882215)
XLA Ops:
  0.6 5.1 %weigh.1 = (f32[104,128]{1,0:T(8,128)}, f32[96,128]{1,0:T(8,128)}) custom-call(bf16[1536,1024]{1,0:T(8,128)(2,1)} %desc.1, s32[12,128]{1,0:T(8,128)} %bitcast.9, s32[1,1536]{1,0:T(1,128)} %labels.1, f32[1,24]{1,0:T(1,128)} %bitcast.12, bf16[512,1024]{1,0:T(8,128)(2,1)} %points.1, s32[1,512]{1,0:T(1,128)} %bitcast.10), custom_call_target="tpu_custom_call" | custom-call | flops 1610612736 | bytes 4194304 | tf_op jit(solution)/shard_map/weigh/pallas_call | solution.py:142
  5.7 9.1 %collective-permute-start = (f32[104,128]{1,0:T(8,128)}, f32[104,128]{1,0:T(8,128)S(1)}, u32[]{:S(2)}, u32[]{:S(2)}) collective-permute-start(f32[104,128]{1,0:T(8,128)} %get-tuple-element.8.first), channel_id=1, source_target_pairs={{0,256},{1,257},{2,258},{3,259},{4,260},{5,261},{6,262},{7,263},{8... | collective-permute-start | bytes 159752 | tf_op jit(solution)/shard_map/ppermute | solution.py:35
  14.8 7.9 %collective-permute-start.4 = (f32[96,128]{1,0:T(8,128)}, f32[96,128]{1,0:T(8,128)S(1)}, u32[]{:S(2)}, u32[]{:S(2)}) collective-permute-start(f32[96,128]{1,0:T(8,128)} %get-tuple-element.9), channel_id=1, source_target_pairs={{0,1},{1,65},{2,129},{3,193},{4,257},{5,321},{6,385},{7,449},{8,9}... | collective-permute-start | bytes 147464 | tf_op jit(solution)/shard_map/ppermute | solution.py:35
  22.7 7.6 %collective-permute-start.3 = (f32[96,128]{1,0:T(8,128)}, f32[96,128]{1,0:T(8,128)S(1)}, u32[]{:S(2)}, u32[]{:S(2)}) collective-permute-start(f32[96,128]{1,0:T(8,128)} %get-tuple-element.9), channel_id=1, source_target_pairs={{0,0},{1,64},{2,128},{3,192},{4,256},{5,320},{6,384},{7,448},{8,8}... | collective-permute-start | bytes 147464 | tf_op jit(solution)/shard_map/ppermute | solution.py:35
  30.3 0.0 collective-permute-done.second
  30.3 0.0 copy-start
  30.4 0.8 %copy-done = f32[104,128]{1,0:T(8,128)S(1)} copy-done((f32[104,128]{1,0:T(8,128)S(1)}, f32[104,128]{1,0:T(8,128)}, u32[]{:S(2)}) %copy-start) | copy-done | bytes 53272
  31.2 3.7 %collective-permute-start.1 = (f32[2,104,128]{2,1,0:T(8,128)S(1)}, f32[2,104,128]{2,1,0:T(8,128)S(1)}, u32[]{:S(2)}, u32[]{:S(2)}) collective-permute-start(f32[2,104,128]{2,1,0:T(8,128)S(1)} %pack_a_two.1.first), channel_id=1, source_target_pairs={{0,128},{1,129},{2,130},{3,131},{4,132},{5,133},{6,134},{7,135},{8... | collective-permute-start | bytes 319496 | tf_op jit(solution)/shard_map/ppermute | solution.py:35
  34.8 0.0 collective-permute-done.4.second
  34.9 1.9 %collective-permute-done.3.first = f32[96,128]{1,0:T(8,128)S(1)} collective-permute-done((f32[96,128]{1,0:T(8,128)}, f32[96,128]{1,0:T(8,128)S(1)}, u32[]{:S(2)}, u32[]{:S(2)}) %collective-permute-start.3) | collective-permute-done | bytes 49184 | tf_op jit(solution)/shard_map/ppermute | solution.py:35
  36.8 2.2 %collective-permute-start.5 = (f32[2,96,128]{2,1,0:T(8,128)S(1)}, f32[2,96,128]{2,1,0:T(8,128)S(1)}, u32[]{:S(2)}, u32[]{:S(2)}) collective-permute-start(f32[2,96,128]{2,1,0:T(8,128)S(1)} %pack_b_two.1.first), channel_id=1, source_target_pairs={{0,2},{1,3},{2,0},{3,1},{4,6},{5,7},{6,4},{7,5},{8,10},{9,11},{10,... | collective-permute-start | bytes 294920 | tf_op jit(solution)/shard_map/ppermute | solution.py:35
  39.0 1.1 %collective-permute-done.1.second = f32[2,104,128]{2,1,0:T(8,128)S(1)} collective-permute-done((f32[2,104,128]{2,1,0:T(8,128)S(1)}, f32[2,104,128]{2,1,0:T(8,128)S(1)}, u32[]{:S(2)}, u32[]{:S(2)}) %collective-permute-start.1) | collective-permute-done | bytes 106528 | tf_op jit(solution)/shard_map/ppermute | solution.py:35
  40.1 1.9 %collective-permute-start.2 = (f32[4,104,128]{2,1,0:T(8,128)S(1)}, f32[4,104,128]{2,1,0:T(8,128)S(1)}, u32[]{:S(2)}, u32[]{:S(2)}) collective-permute-start(f32[4,104,128]{2,1,0:T(8,128)S(1)} %pack_a_four.1.a0), channel_id=1, source_target_pairs={{0,64},{1,65},{2,66},{3,67},{4,68},{5,69},{6,70},{7,71},{8,72},{9,... | collective-permute-start | bytes 638984 | tf_op jit(solution)/shard_map/ppermute | solution.py:35
  42.1 1.2 %collective-permute-done.5.second = f32[2,96,128]{2,1,0:T(8,128)S(1)} collective-permute-done((f32[2,96,128]{2,1,0:T(8,128)S(1)}, f32[2,96,128]{2,1,0:T(8,128)S(1)}, u32[]{:S(2)}, u32[]{:S(2)}) %collective-permute-start.5) | collective-permute-done | bytes 98336 | tf_op jit(solution)/shard_map/ppermute | solution.py:35
  43.3 1.9 %collective-permute-start.6 = (f32[4,96,128]{2,1,0:T(8,128)S(1)}, f32[4,96,128]{2,1,0:T(8,128)S(1)}, u32[]{:S(2)}, u32[]{:S(2)}) collective-permute-start(f32[4,96,128]{2,1,0:T(8,128)S(1)} %pack_b_four.1.b0), channel_id=1, source_target_pairs={{0,6},{1,7},{2,4},{3,5},{4,2},{5,3},{6,0},{7,1},{8,14},{9,15},{10,... | collective-permute-start | bytes 589832 | tf_op jit(solution)/shard_map/ppermute | solution.py:35
  45.3 0.1 pad_add_fusion.where
  45.4 6.7 %collective-permute-done.6.b1 = f32[4,96,128]{2,1,0:T(8,128)S(1)} collective-permute-done((f32[4,96,128]{2,1,0:T(8,128)S(1)}, f32[4,96,128]{2,1,0:T(8,128)S(1)}, u32[]{:S(2)}, u32[]{:S(2)}) %collective-permute-start.6) | collective-permute-done | bytes 196640 | tf_op jit(solution)/shard_map/ppermute | solution.py:35
  52.1 0.0 collective-permute-done.2.a1
  52.1 1.3 %tile.1 = (f32[1032,128]{1,0:T(8,128)S(1)}, f32[1032,128]{1,0:T(8,128)S(1)}) custom-call(s32[3]{0:T(128)S(1)} %pad_add_fusion.where, f32[4,104,128]{2,1,0:T(8,128)S(1)} %pack_a_four.1.a0, f32[4,104,128]{2,1,0:T(8,128)S(1)} %collective-permute-done.2.a1, f32[4,96,128]{2,1,0:T(8,128)S(1)} %pack_b_four.1.b0, f32[4,96,128]{2,1,0:T(8,128)S(1)} %collective-permute-done.6.b1), custom_call_target="tpu_custom_call" | custom-call | flops 301989888 | bytes 1875980 | tf_op jit(solution)/shard_map/tile/pallas_call | solution.py:159
  53.4 1.9 %collective-permute-start.7 = (f32[1032,128]{1,0:T(8,128)S(1)}, f32[1032,128]{1,0:T(8,128)S(1)}, u32[]{:S(2)}, u32[]{:S(2)}) collective-permute-start(f32[1032,128]{1,0:T(8,128)S(1)} %get-tuple-element.11), channel_id=1, source_target_pairs={{0,8},{1,9},{2,10},{3,11},{4,12},{5,13},{6,14},{7,15},{8,0},{9,1},... | collective-permute-start | bytes 1585160 | tf_op jit(solution)/shard_map/ppermute | solution.py:35
  55.3 1.9 %collective-permute-done.7.got = f32[1032,128]{1,0:T(8,128)S(1)} collective-permute-done((f32[1032,128]{1,0:T(8,128)S(1)}, f32[1032,128]{1,0:T(8,128)S(1)}, u32[]{:S(2)}, u32[]{:S(2)}) %collective-permute-start.7) | collective-permute-done | bytes 528416 | tf_op jit(solution)/shard_map/ppermute | solution.py:35
  57.2 0.1 scatter.1
  57.2 14.0 %all_to_all.5.came = f32[4,264,128]{2,1,0:T(8,128)S(1)} all-to-all(f32[4,264,128]{2,1,0:T(8,128)S(1)} %scatter.1), channel_id=1, replica_groups={{0,16,32,48},{1,17,33,49},{2,18,34,50},{3,19,35,51},{4,20,36,52},{5,21,..., dimensions={0} | all-to-all | bytes 1081344 | tf_op jit(solution)/shard_map/all_to_all | solution.py:289
  71.3 0.7 last.1
  (4 shorter events, 0.0 us)
Async XLA Ops:
  5.7 24.6 %collective-permute-start = (f32[104,128]{1,0:T(8,128)}, f32[104,128]{1,0:T(8,128)S(1)}, u32[]{:S(2)}, u32[]{:S(2)}) collective-permute-start(f32[104,128]{1,0:T(8,128)} %get-tuple-element.8.first), channel_id=1, source_target_pairs={{0,256},{1,257},{2,258},{3,259},{4,260},{5,261},{6,262},{7,263},{8... | collective-permute-start | bytes 159752 | tf_op jit(solution)/shard_map/ppermute | solution.py:35
  14.8 20.0 %collective-permute-start.4 = (f32[96,128]{1,0:T(8,128)}, f32[96,128]{1,0:T(8,128)S(1)}, u32[]{:S(2)}, u32[]{:S(2)}) collective-permute-start(f32[96,128]{1,0:T(8,128)} %get-tuple-element.9), channel_id=1, source_target_pairs={{0,1},{1,65},{2,129},{3,193},{4,257},{5,321},{6,385},{7,449},{8,9}... | collective-permute-start | bytes 147464 | tf_op jit(solution)/shard_map/ppermute | solution.py:35
  22.7 14.1 %collective-permute-start.3 = (f32[96,128]{1,0:T(8,128)}, f32[96,128]{1,0:T(8,128)S(1)}, u32[]{:S(2)}, u32[]{:S(2)}) collective-permute-start(f32[96,128]{1,0:T(8,128)} %get-tuple-element.9), channel_id=1, source_target_pairs={{0,0},{1,64},{2,128},{3,192},{4,256},{5,320},{6,384},{7,448},{8,8}... | collective-permute-start | bytes 147464 | tf_op jit(solution)/shard_map/ppermute | solution.py:35
  30.3 0.8 %copy-start = (f32[104,128]{1,0:T(8,128)S(1)}, f32[104,128]{1,0:T(8,128)}, u32[]{:S(2)}) copy-start(f32[104,128]{1,0:T(8,128)} %get-tuple-element.8.first) | copy-start | bytes 159748
  31.2 8.9 %collective-permute-start.1 = (f32[2,104,128]{2,1,0:T(8,128)S(1)}, f32[2,104,128]{2,1,0:T(8,128)S(1)}, u32[]{:S(2)}, u32[]{:S(2)}) collective-permute-start(f32[2,104,128]{2,1,0:T(8,128)S(1)} %pack_a_two.1.first), channel_id=1, source_target_pairs={{0,128},{1,129},{2,130},{3,131},{4,132},{5,133},{6,134},{7,135},{8... | collective-permute-start | bytes 319496 | tf_op jit(solution)/shard_map/ppermute | solution.py:35
  36.8 6.5 %collective-permute-start.5 = (f32[2,96,128]{2,1,0:T(8,128)S(1)}, f32[2,96,128]{2,1,0:T(8,128)S(1)}, u32[]{:S(2)}, u32[]{:S(2)}) collective-permute-start(f32[2,96,128]{2,1,0:T(8,128)S(1)} %pack_b_two.1.first), channel_id=1, source_target_pairs={{0,2},{1,3},{2,0},{3,1},{4,6},{5,7},{6,4},{7,5},{8,10},{9,11},{10,... | collective-permute-start | bytes 294920 | tf_op jit(solution)/shard_map/ppermute | solution.py:35
  40.1 12.0 %collective-permute-start.2 = (f32[4,104,128]{2,1,0:T(8,128)S(1)}, f32[4,104,128]{2,1,0:T(8,128)S(1)}, u32[]{:S(2)}, u32[]{:S(2)}) collective-permute-start(f32[4,104,128]{2,1,0:T(8,128)S(1)} %pack_a_four.1.a0), channel_id=1, source_target_pairs={{0,64},{1,65},{2,66},{3,67},{4,68},{5,69},{6,70},{7,71},{8,72},{9,... | collective-permute-start | bytes 638984 | tf_op jit(solution)/shard_map/ppermute | solution.py:35
  43.3 8.8 %collective-permute-start.6 = (f32[4,96,128]{2,1,0:T(8,128)S(1)}, f32[4,96,128]{2,1,0:T(8,128)S(1)}, u32[]{:S(2)}, u32[]{:S(2)}) collective-permute-start(f32[4,96,128]{2,1,0:T(8,128)S(1)} %pack_b_four.1.b0), channel_id=1, source_target_pairs={{0,6},{1,7},{2,4},{3,5},{4,2},{5,3},{6,0},{7,1},{8,14},{9,15},{10,... | collective-permute-start | bytes 589832 | tf_op jit(solution)/shard_map/ppermute | solution.py:35
  53.4 3.8 %collective-permute-start.7 = (f32[1032,128]{1,0:T(8,128)S(1)}, f32[1032,128]{1,0:T(8,128)S(1)}, u32[]{:S(2)}, u32[]{:S(2)}) collective-permute-start(f32[1032,128]{1,0:T(8,128)S(1)} %get-tuple-element.11), channel_id=1, source_target_pairs={{0,8},{1,9},{2,10},{3,11},{4,12},{5,13},{6,14},{7,15},{8,0},{9,1},... | collective-permute-start | bytes 1585160 | tf_op jit(solution)/shard_map/ppermute | solution.py:35

commit v4 on v3

--- a/solution.py
+++ b/solution.py
@@ -185,16 +185,16 @@
 A_ORDER = (0, 4, 2, 6, 1, 5, 3, 7)
 
 
-def tile(structs, owned, where, a0, a1, b0, b1, give, keep, a_all, b_all, b_rows, product):
+def tile(structs, owned, where, a0, a1, b_lanes, give, keep, a_all, b_all, b_rows, product):
     cols = a_all.shape[1]
-    for j in range(4):
-        b_rows[j], b_rows[j ^ 6] = b0[j], b1[j]
-    swap, core = where[0], where[1]
+    for j in range(Y):
+        b_rows[2 * j], b_rows[2 * j + 1] = b_lanes[j, 0], b_lanes[j, 1]
+    k, zh, core = where[0], where[1], where[2]
     rhs = jnp.zeros((8, LANES), F32)
     for p, m in enumerate(A_ORDER):
         a = (a0 if p < 4 else a1).at[p % 4]
         rhs = rhs + a[4 * structs :]
-        b = b_rows.at[jnp.bitwise_xor(swap, m)]
+        b = b_rows.at[(k ^ m) ^ zh]
         for j in range(cols // LANES):
             block = (pl.ds(p * structs, structs), pl.ds(j * LANES, LANES))
             a_all[block] = a[j * structs : (j + 1) * structs]
@@ -233,6 +233,15 @@
     rhs[...] = jnp.concatenate([tail[j : j + 1] for j in range(4)], axis=1)
 
 
+def repeat(first, second, out):
+    for j in range(Y):
+        out[j, 0], out[j, 1] = first[...], second[...]
+
+
+def y_groups():
+    return [[e * Y * ZH + y * ZH + h for y in range(Y)] for e in range(ZL * X * C) for h in range(ZH)]
+
+
 def x_groups():
     return [
         [((z * X + x) * C + c) * Y * ZH + s for x in range(X)]
@@ -246,7 +255,7 @@
     structs, cols = energies.shape[0], sparse_points.shape[0]
     owned = cols // (X * C)
     env, sp = lax.axis_index("env"), lax.axis_index("sp")
-    where = jnp.stack([(env // (X * C)) ^ sp, env % C, env // C % X]).astype(jnp.int32)
+    where = jnp.stack([env // (X * C), sp % ZH, env % C]).astype(jnp.int32)
 
     wire, cut = weigh_call(
         descriptors,
@@ -263,17 +272,15 @@
     t1 = send(cut, turned(1))
     a_two = join(wire, far, "pack_a_two")
     a_got = send(a_two, over_z(2))
-    b_two = join(t0, t1, "pack_b_two")
-    b_got = send(b_two, over_y(1))
+    (b_own,) = simple(repeat, [(Y, 2, rows, LANES)], [t0, t1], name="repeat")
+    b_all = lax.all_to_all(b_own, AXES, 0, 0, axis_index_groups=y_groups())
     a_four = join(a_two, a_got, "pack_a_four")
     a_more = send(a_four, over_z(1))
-    b_four = join(b_two, b_got, "pack_b_four")
-    b_more = send(b_four, over_y(3))
     piece = owned * (cols // LANES)
     give, keep = simple(
         functools.partial(tile, structs, owned),
         [(X * piece + 8, LANES)] * 2,
-        [where, a_four, a_more, b_four, b_more],
+        [where, a_four, a_more, b_all],
         scratch=[
             pltpu.VMEM((8 * structs, cols), F32),
             pltpu.VMEM((8 * structs, cols), F32),

time: 72.4 us -> 70.4 us (0.972)
  waiting for transfers between devices: 12.8 us -> 9.51 us
  Pallas kernels: 7.12 us -> 7.87 us
    ppermute x8 -> x6, waiting for transfers between devices: 12.8 us -> 6.25 us  [send(): return lax.ppermute(value, AXES, pairs(move))]
    all_to_all x0 -> x1, starting transfers between devices: none -> 4.5 us  [local(): b_all = lax.all_to_all(b_own, AXES, 0, 0, axis_index_groups=y_groups())]
    ppermute x8 -> x6, starting transfers between devices: 36.3 us -> 32.1 us  [send(): return lax.ppermute(value, AXES, pairs(move))]
    all_to_all x0 -> x1, waiting for transfers between devices: none -> 3.26 us  [local(): b_all = lax.all_to_all(b_own, AXES, 0, 0, axis_index_groups=y_groups())]
    pallas_call x7 -> x6, Pallas kernels: 2.05 us -> 2.8 us  [simple(): pl.pallas_call(kernel, out_shape=[jax.ShapeDtypeStruct(s, F32) for s in s...]
  transfers between devices with their start and end apart: 8 -> 7, of which waited for: 5 -> 4; matrix products, arithmetic and copies ran while one was open for 0% -> 0% of each run, Pallas kernels for 0% -> 1%
where the time goes in v4:
time: 70.4 us; the launch traced here: 69.7 us
  starting transfers between devices  36.6 us (52%)
  blocking collectives  14 us (20%)
  waiting for transfers between devices  9.51 us (14%)
  Pallas kernels  7.87 us (11%)
  local copies, waits for them, and re-layouts  0.8 us (1%)
  between operations  0.76 us (1%)
    ppermute x6, starting transfers between devices, send(): return lax.ppermute(value, AXES, pairs(move))  32.1 us
    all_to_all x1, blocking collectives, local(): came = lax.all_to_all(parts, AXES, 0, 0, axis_index_groups=x_groups())  14 us
    ppermute x6, waiting for transfers between devices, send(): return lax.ppermute(value, AXES, pairs(move))  6.25 us
    pallas_call x1, Pallas kernels, weigh_call(): pl.pallas_call(functools.partial(weigh, chunks, total), in_specs=[pl.Bloc...  5.07 us
    all_to_all x1, starting transfers between devices, local(): b_all = lax.all_to_all(b_own, AXES, 0, 0, axis_index_groups=y_groups())  4.5 us
    all_to_all x1, waiting for transfers between devices, local(): b_all = lax.all_to_all(b_own, AXES, 0, 0, axis_index_groups=y_groups())  3.26 us
    pallas_call x6, Pallas kernels, simple(): pl.pallas_call(kernel, out_shape=[jax.ShapeDtypeStruct(s, F32) for s in s...  2.8 us
  transfers between devices with their start and end apart: 7, of which 4 were waited for; matrix products, arithmetic and copies ran while one was open for 0% of the time, Pallas kernels for 1%

profile of v4, /device:TPU:24, one launch (start us, length us, event | category | flops | bytes accessed | tf_op | source)
XLA Modules:
  0.0 69.7 jit_solution(279453500841498865)
XLA Ops:
  0.6 5.1 %weigh.1 = (f32[104,128]{1,0:T(8,128)}, f32[96,128]{1,0:T(8,128)}) custom-call(bf16[1536,1024]{1,0:T(8,128)(2,1)} %desc.1, s32[12,128]{1,0:T(8,128)} %bitcast.9, s32[1,1536]{1,0:T(1,128)} %labels.1, f32[1,24]{1,0:T(1,128)} %bitcast.12, bf16[512,1024]{1,0:T(8,128)(2,1)} %points.1, s32[1,512]{1,0:T(1,128)} %bitcast.10), custom_call_target="tpu_custom_call" | custom-call | flops 1610612736 | bytes 4194304 | tf_op jit(solution)/shard_map/weigh/pallas_call | solution.py:142
  5.7 9.1 %collective-permute-start = (f32[104,128]{1,0:T(8,128)}, f32[104,128]{1,0:T(8,128)S(1)}, u32[]{:S(2)}, u32[]{:S(2)}) collective-permute-start(f32[104,128]{1,0:T(8,128)} %get-tuple-element.8.first), channel_id=1, source_target_pairs={{0,256},{1,257},{2,258},{3,259},{4,260},{5,261},{6,262},{7,263},{8... | collective-permute-start | bytes 159752 | tf_op jit(solution)/shard_map/ppermute | solution.py:35
  14.8 7.9 %collective-permute-start.4 = (f32[96,128]{1,0:T(8,128)}, f32[96,128]{1,0:T(8,128)S(1)}, u32[]{:S(2)}, u32[]{:S(2)}) collective-permute-start(f32[96,128]{1,0:T(8,128)} %get-tuple-element.9), channel_id=1, source_target_pairs={{0,1},{1,65},{2,129},{3,193},{4,257},{5,321},{6,385},{7,449},{8,9}... | collective-permute-start | bytes 147464 | tf_op jit(solution)/shard_map/ppermute | solution.py:35
  22.7 7.6 %collective-permute-start.3 = (f32[96,128]{1,0:T(8,128)}, f32[96,128]{1,0:T(8,128)S(1)}, u32[]{:S(2)}, u32[]{:S(2)}) collective-permute-start(f32[96,128]{1,0:T(8,128)} %get-tuple-element.9), channel_id=1, source_target_pairs={{0,0},{1,64},{2,128},{3,192},{4,256},{5,320},{6,384},{7,448},{8,8}... | collective-permute-start | bytes 147464 | tf_op jit(solution)/shard_map/ppermute | solution.py:35
  30.3 0.0 collective-permute-done.second
  30.3 0.0 copy-start
  30.4 0.8 %copy-done = f32[104,128]{1,0:T(8,128)S(1)} copy-done((f32[104,128]{1,0:T(8,128)S(1)}, f32[104,128]{1,0:T(8,128)}, u32[]{:S(2)}) %copy-start) | copy-done | bytes 53272
  31.2 3.7 %collective-permute-start.1 = (f32[2,104,128]{2,1,0:T(8,128)S(1)}, f32[2,104,128]{2,1,0:T(8,128)S(1)}, u32[]{:S(2)}, u32[]{:S(2)}) collective-permute-start(f32[2,104,128]{2,1,0:T(8,128)S(1)} %pack_a_two.1.first), channel_id=1, source_target_pairs={{0,128},{1,129},{2,130},{3,131},{4,132},{5,133},{6,134},{7,135},{8... | collective-permute-start | bytes 319496 | tf_op jit(solution)/shard_map/ppermute | solution.py:35
  34.8 0.0 collective-permute-done.4.second
  34.9 1.9 %collective-permute-done.3.first = f32[96,128]{1,0:T(8,128)S(1)} collective-permute-done((f32[96,128]{1,0:T(8,128)}, f32[96,128]{1,0:T(8,128)S(1)}, u32[]{:S(2)}, u32[]{:S(2)}) %collective-permute-start.3) | collective-permute-done | bytes 49184 | tf_op jit(solution)/shard_map/ppermute | solution.py:35
  36.8 0.8 %repeat.1 = f32[4,2,96,128]{3,2,1,0:T(8,128)} custom-call(f32[96,128]{1,0:T(8,128)S(1)} %collective-permute-done.3.first, f32[96,128]{1,0:T(8,128)S(1)} %collective-permute-done.4.second), custom_call_target="tpu_custom_call" | custom-call | bytes 491520 | tf_op jit(solution)/shard_map/repeat/pallas_call | solution.py:159
  37.5 4.5 %all-to-all-start = ((f32[4,2,96,128]{3,2,1,0:T(8,128)}), f32[4,2,96,128]{3,2,1,0:T(8,128)S(1)}, u32[]{:S(2)}, u32[]{:S(2)}) async-start(f32[4,2,96,128]{3,2,1,0:T(8,128)} %repeat.1), calls=%async_computation | async-start | bytes 786432 | tf_op jit(solution)/shard_map/all_to_all | solution.py:276
  42.0 0.0 collective-permute-done.1.second
  42.1 1.9 %collective-permute-start.2 = (f32[4,104,128]{2,1,0:T(8,128)S(1)}, f32[4,104,128]{2,1,0:T(8,128)S(1)}, u32[]{:S(2)}, u32[]{:S(2)}) collective-permute-start(f32[4,104,128]{2,1,0:T(8,128)S(1)} %pack_a_four.1.a0), channel_id=1, source_target_pairs={{0,64},{1,65},{2,66},{3,67},{4,68},{5,69},{6,70},{7,71},{8,72},{9,... | collective-permute-start | bytes 638984 | tf_op jit(solution)/shard_map/ppermute | solution.py:35
  44.0 0.1 pad_add_fusion.where
  44.1 3.3 %all-to-all-done.b_lanes = f32[4,2,96,128]{3,2,1,0:T(8,128)S(1)} async-done(((f32[4,2,96,128]{3,2,1,0:T(8,128)}), f32[4,2,96,128]{3,2,1,0:T(8,128)S(1)}, u32[]{:S(2)}, u32[]{:S(2)}) %all-to-all-start) | async-done | bytes 393248 | tf_op jit(solution)/shard_map/all_to_all | solution.py:276
  47.4 2.4 %collective-permute-done.2.a1 = f32[4,104,128]{2,1,0:T(8,128)S(1)} collective-permute-done((f32[4,104,128]{2,1,0:T(8,128)S(1)}, f32[4,104,128]{2,1,0:T(8,128)S(1)}, u32[]{:S(2)}, u32[]{:S(2)}) %collective-permute-start.2) | collective-permute-done | bytes 213024 | tf_op jit(solution)/shard_map/ppermute | solution.py:35
  49.8 1.3 %tile.1 = (f32[1032,128]{1,0:T(8,128)S(1)}, f32[1032,128]{1,0:T(8,128)S(1)}) custom-call(s32[3]{0:T(128)S(1)} %pad_add_fusion.where, f32[4,104,128]{2,1,0:T(8,128)S(1)} %pack_a_four.1.a0, f32[4,104,128]{2,1,0:T(8,128)S(1)} %collective-permute-done.2.a1, f32[4,2,96,128]{3,2,1,0:T(8,128)S(1)} %all-to-all-done.b_lanes), custom_call_target="tpu_custom_call" | custom-call | flops 301989888 | bytes 1875980 | tf_op jit(solution)/shard_map/tile/pallas_call | solution.py:159
  51.1 1.9 %collective-permute-start.5 = (f32[1032,128]{1,0:T(8,128)S(1)}, f32[1032,128]{1,0:T(8,128)S(1)}, u32[]{:S(2)}, u32[]{:S(2)}) collective-permute-start(f32[1032,128]{1,0:T(8,128)S(1)} %get-tuple-element.11), channel_id=1, source_target_pairs={{0,8},{1,9},{2,10},{3,11},{4,12},{5,13},{6,14},{7,15},{8,0},{9,1},... | collective-permute-start | bytes 1585160 | tf_op jit(solution)/shard_map/ppermute | solution.py:35
  53.0 1.9 %collective-permute-done.5.got = f32[1032,128]{1,0:T(8,128)S(1)} collective-permute-done((f32[1032,128]{1,0:T(8,128)S(1)}, f32[1032,128]{1,0:T(8,128)S(1)}, u32[]{:S(2)}, u32[]{:S(2)}) %collective-permute-start.5) | collective-permute-done | bytes 528416 | tf_op jit(solution)/shard_map/ppermute | solution.py:35
  54.9 0.1 scatter.1
  55.0 14.0 %all_to_all.10.came = f32[4,264,128]{2,1,0:T(8,128)S(1)} all-to-all(f32[4,264,128]{2,1,0:T(8,128)S(1)} %scatter.1), channel_id=1, replica_groups={{0,16,32,48},{1,17,33,49},{2,18,34,50},{3,19,35,51},{4,20,36,52},{5,21,..., dimensions={0} | all-to-all | bytes 1081344 | tf_op jit(solution)/shard_map/all_to_all | solution.py:296
  69.0 0.7 last.1
  (2 shorter events, 0.0 us)
Async XLA Ops:
  5.7 24.6 %collective-permute-start = (f32[104,128]{1,0:T(8,128)}, f32[104,128]{1,0:T(8,128)S(1)}, u32[]{:S(2)}, u32[]{:S(2)}) collective-permute-start(f32[104,128]{1,0:T(8,128)} %get-tuple-element.8.first), channel_id=1, source_target_pairs={{0,256},{1,257},{2,258},{3,259},{4,260},{5,261},{6,262},{7,263},{8... | collective-permute-start | bytes 159752 | tf_op jit(solution)/shard_map/ppermute | solution.py:35
  14.8 20.0 %collective-permute-start.4 = (f32[96,128]{1,0:T(8,128)}, f32[96,128]{1,0:T(8,128)S(1)}, u32[]{:S(2)}, u32[]{:S(2)}) collective-permute-start(f32[96,128]{1,0:T(8,128)} %get-tuple-element.9), channel_id=1, source_target_pairs={{0,1},{1,65},{2,129},{3,193},{4,257},{5,321},{6,385},{7,449},{8,9}... | collective-permute-start | bytes 147464 | tf_op jit(solution)/shard_map/ppermute | solution.py:35
  22.7 14.1 %collective-permute-start.3 = (f32[96,128]{1,0:T(8,128)}, f32[96,128]{1,0:T(8,128)S(1)}, u32[]{:S(2)}, u32[]{:S(2)}) collective-permute-start(f32[96,128]{1,0:T(8,128)} %get-tuple-element.9), channel_id=1, source_target_pairs={{0,0},{1,64},{2,128},{3,192},{4,256},{5,320},{6,384},{7,448},{8,8}... | collective-permute-start | bytes 147464 | tf_op jit(solution)/shard_map/ppermute | solution.py:35
  30.3 0.8 %copy-start = (f32[104,128]{1,0:T(8,128)S(1)}, f32[104,128]{1,0:T(8,128)}, u32[]{:S(2)}) copy-start(f32[104,128]{1,0:T(8,128)} %get-tuple-element.8.first) | copy-start | bytes 159748
  31.2 10.9 %collective-permute-start.1 = (f32[2,104,128]{2,1,0:T(8,128)S(1)}, f32[2,104,128]{2,1,0:T(8,128)S(1)}, u32[]{:S(2)}, u32[]{:S(2)}) collective-permute-start(f32[2,104,128]{2,1,0:T(8,128)S(1)} %pack_a_two.1.first), channel_id=1, source_target_pairs={{0,128},{1,129},{2,130},{3,131},{4,132},{5,133},{6,134},{7,135},{8... | collective-permute-start | bytes 319496 | tf_op jit(solution)/shard_map/ppermute | solution.py:35
  37.5 9.8 %all-to-all-start = ((f32[4,2,96,128]{3,2,1,0:T(8,128)}), f32[4,2,96,128]{3,2,1,0:T(8,128)S(1)}, u32[]{:S(2)}, u32[]{:S(2)}) async-start(f32[4,2,96,128]{3,2,1,0:T(8,128)} %repeat.1), calls=%async_computation | async-start | bytes 786432 | tf_op jit(solution)/shard_map/all_to_all | solution.py:276
  42.1 7.7 %collective-permute-start.2 = (f32[4,104,128]{2,1,0:T(8,128)S(1)}, f32[4,104,128]{2,1,0:T(8,128)S(1)}, u32[]{:S(2)}, u32[]{:S(2)}) collective-permute-start(f32[4,104,128]{2,1,0:T(8,128)S(1)} %pack_a_four.1.a0), channel_id=1, source_target_pairs={{0,64},{1,65},{2,66},{3,67},{4,68},{5,69},{6,70},{7,71},{8,72},{9,... | collective-permute-start | bytes 638984 | tf_op jit(solution)/shard_map/ppermute | solution.py:35
  51.1 3.8 %collective-permute-start.5 = (f32[1032,128]{1,0:T(8,128)S(1)}, f32[1032,128]{1,0:T(8,128)S(1)}, u32[]{:S(2)}, u32[]{:S(2)}) collective-permute-start(f32[1032,128]{1,0:T(8,128)S(1)} %get-tuple-element.11), channel_id=1, source_target_pairs={{0,8},{1,9},{2,10},{3,11},{4,12},{5,13},{6,14},{7,15},{8,0},{9,1},... | collective-permute-start | bytes 1585160 | tf_op jit(solution)/shard_map/ppermute | solution.py:35

commit v5 on v4

--- a/solution.py
+++ b/solution.py
@@ -51,8 +51,16 @@
     return (zl, x, 1 - c, y, zh)
 
 
+def nearer(k, q):
+    return (k - q > 2) | ((k - q == 2) & (k < Y))
+
+
 def turned(flip):
-    return lambda zl, x, c, y, zh: (y * ZH + zh, x, c, zl // ZH, (zl % ZH) ^ flip)
+    def move(zl, x, c, y, zh):
+        k, q, upper = y * ZH + zh, zl % Y, zl // Y
+        return (k, x, c, q, zh ^ upper ^ flip ^ int(nearer(k, q)))
+
+    return move
 
 
 def halves(value):
@@ -194,7 +202,9 @@
     for p, m in enumerate(A_ORDER):
         a = (a0 if p < 4 else a1).at[p % 4]
         rhs = rhs + a[4 * structs :]
-        b = b_rows.at[(k ^ m) ^ zh]
+        lane = (k ^ m) & (Y - 1)
+        slot = ((k ^ m) // Y) ^ zh ^ (k & 1) ^ nearer(k, lane).astype(jnp.int32)
+        b = b_rows.at[2 * lane + slot]
         for j in range(cols // LANES):
             block = (pl.ds(p * structs, structs), pl.ds(j * LANES, LANES))
             a_all[block] = a[j * structs : (j + 1) * structs]

time: 70.4 us -> 70.2 us (level)
  the two profiles are of different devices: /device:TPU:24 before, /device:TPU:104 now
where the time goes in v5:
time: 70.2 us; the launch traced here: 69.8 us
  starting transfers between devices  32.2 us (46%)
  waiting for transfers between devices  14 us (20%)
  blocking collectives  14 us (20%)
  Pallas kernels  7.91 us (11%)
  local copies, waits for them, and re-layouts  0.8 us (1%)
  between operations  0.76 us (1%)
    ppermute x6, starting transfers between devices, send(): return lax.ppermute(value, AXES, pairs(move))  28.5 us
    all_to_all x1, blocking collectives, local(): came = lax.all_to_all(parts, AXES, 0, 0, axis_index_groups=x_groups())  14 us
    ppermute x6, waiting for transfers between devices, send(): return lax.ppermute(value, AXES, pairs(move))  10.1 us
    pallas_call x1, Pallas kernels, weigh_call(): pl.pallas_call(functools.partial(weigh, chunks, total), in_specs=[pl.Bloc...  5.08 us
    all_to_all x1, waiting for transfers between devices, local(): b_all = lax.all_to_all(b_own, AXES, 0, 0, axis_index_groups=y_groups())  3.87 us
    all_to_all x1, starting transfers between devices, local(): b_all = lax.all_to_all(b_own, AXES, 0, 0, axis_index_groups=y_groups())  3.76 us
    pallas_call x6, Pallas kernels, simple(): pl.pallas_call(kernel, out_shape=[jax.ShapeDtypeStruct(s, F32) for s in s...  2.84 us
  transfers between devices with their start and end apart: 7, of which 4 were waited for; matrix products, arithmetic and copies ran while one was open for 0% of the time, Pallas kernels for 1%

profile of v5, /device:TPU:104, one launch (start us, length us, event | category | flops | bytes accessed | tf_op | source)
XLA Modules:
  0.0 69.8 jit_solution(16582243780304484135)
XLA Ops:
  0.6 5.1 %weigh.1 = (f32[104,128]{1,0:T(8,128)}, f32[96,128]{1,0:T(8,128)}) custom-call(bf16[1536,1024]{1,0:T(8,128)(2,1)} %desc.1, s32[12,128]{1,0:T(8,128)} %bitcast.9, s32[1,1536]{1,0:T(1,128)} %labels.1, f32[1,24]{1,0:T(1,128)} %bitcast.12, bf16[512,1024]{1,0:T(8,128)(2,1)} %points.1, s32[1,512]{1,0:T(1,128)} %bitcast.10), custom_call_target="tpu_custom_call" | custom-call | flops 1610612736 | bytes 4194304 | tf_op jit(solution)/shard_map/weigh/pallas_call | solution.py:150
  5.7 9.1 %collective-permute-start = (f32[104,128]{1,0:T(8,128)}, f32[104,128]{1,0:T(8,128)S(1)}, u32[]{:S(2)}, u32[]{:S(2)}) collective-permute-start(f32[104,128]{1,0:T(8,128)} %get-tuple-element.8.first), channel_id=1, source_target_pairs={{0,256},{1,257},{2,258},{3,259},{4,260},{5,261},{6,262},{7,263},{8... | collective-permute-start | bytes 159752 | tf_op jit(solution)/shard_map/ppermute | solution.py:35
  14.8 9.5 %collective-permute-start.4 = (f32[96,128]{1,0:T(8,128)}, f32[96,128]{1,0:T(8,128)S(1)}, u32[]{:S(2)}, u32[]{:S(2)}) collective-permute-start(f32[96,128]{1,0:T(8,128)} %get-tuple-element.9), channel_id=1, source_target_pairs={{0,1},{1,64},{2,128},{3,193},{4,256},{5,321},{6,384},{7,449},{8,9}... | collective-permute-start | bytes 147464 | tf_op jit(solution)/shard_map/ppermute | solution.py:35
  24.3 1.9 %collective-permute-start.3 = (f32[96,128]{1,0:T(8,128)}, f32[96,128]{1,0:T(8,128)S(1)}, u32[]{:S(2)}, u32[]{:S(2)}) collective-permute-start(f32[96,128]{1,0:T(8,128)} %get-tuple-element.9), channel_id=1, source_target_pairs={{0,0},{1,65},{2,129},{3,192},{4,257},{5,320},{6,385},{7,448},{8,8}... | collective-permute-start | bytes 147464 | tf_op jit(solution)/shard_map/ppermute | solution.py:35
  26.2 0.0 collective-permute-done.second
  26.3 0.0 copy-start
  26.3 0.8 %copy-done = f32[104,128]{1,0:T(8,128)S(1)} copy-done((f32[104,128]{1,0:T(8,128)S(1)}, f32[104,128]{1,0:T(8,128)}, u32[]{:S(2)}) %copy-start) | copy-done | bytes 53272
  27.1 4.1 %collective-permute-start.1 = (f32[2,104,128]{2,1,0:T(8,128)S(1)}, f32[2,104,128]{2,1,0:T(8,128)S(1)}, u32[]{:S(2)}, u32[]{:S(2)}) collective-permute-start(f32[2,104,128]{2,1,0:T(8,128)S(1)} %pack_a_two.1.first), channel_id=1, source_target_pairs={{0,128},{1,129},{2,130},{3,131},{4,132},{5,133},{6,134},{7,135},{8... | collective-permute-start | bytes 319496 | tf_op jit(solution)/shard_map/ppermute | solution.py:35
  31.2 0.0 collective-permute-done.4.second
  31.2 6.4 %collective-permute-done.3.first = f32[96,128]{1,0:T(8,128)S(1)} collective-permute-done((f32[96,128]{1,0:T(8,128)}, f32[96,128]{1,0:T(8,128)S(1)}, u32[]{:S(2)}, u32[]{:S(2)}) %collective-permute-start.3) | collective-permute-done | bytes 49184 | tf_op jit(solution)/shard_map/ppermute | solution.py:35
  37.6 0.8 %repeat.1 = f32[4,2,96,128]{3,2,1,0:T(8,128)} custom-call(f32[96,128]{1,0:T(8,128)S(1)} %collective-permute-done.3.first, f32[96,128]{1,0:T(8,128)S(1)} %collective-permute-done.4.second), custom_call_target="tpu_custom_call" | custom-call | bytes 491520 | tf_op jit(solution)/shard_map/repeat/pallas_call | solution.py:167
  38.4 3.8 %all-to-all-start = ((f32[4,2,96,128]{3,2,1,0:T(8,128)}), f32[4,2,96,128]{3,2,1,0:T(8,128)S(1)}, u32[]{:S(2)}, u32[]{:S(2)}) async-start(f32[4,2,96,128]{3,2,1,0:T(8,128)} %repeat.1), calls=%async_computation | async-start | bytes 786432 | tf_op jit(solution)/shard_map/all_to_all | solution.py:286
  42.1 0.0 collective-permute-done.1.second
  42.1 1.9 %collective-permute-start.2 = (f32[4,104,128]{2,1,0:T(8,128)S(1)}, f32[4,104,128]{2,1,0:T(8,128)S(1)}, u32[]{:S(2)}, u32[]{:S(2)}) collective-permute-start(f32[4,104,128]{2,1,0:T(8,128)S(1)} %pack_a_four.1.a0), channel_id=1, source_target_pairs={{0,64},{1,65},{2,66},{3,67},{4,68},{5,69},{6,70},{7,71},{8,72},{9,... | collective-permute-start | bytes 638984 | tf_op jit(solution)/shard_map/ppermute | solution.py:35
  44.1 0.1 pad_add_fusion.where
  44.2 3.9 %all-to-all-done.b_lanes = f32[4,2,96,128]{3,2,1,0:T(8,128)S(1)} async-done(((f32[4,2,96,128]{3,2,1,0:T(8,128)}), f32[4,2,96,128]{3,2,1,0:T(8,128)S(1)}, u32[]{:S(2)}, u32[]{:S(2)}) %all-to-all-start) | async-done | bytes 393248 | tf_op jit(solution)/shard_map/all_to_all | solution.py:286
  48.0 1.8 %collective-permute-done.2.a1 = f32[4,104,128]{2,1,0:T(8,128)S(1)} collective-permute-done((f32[4,104,128]{2,1,0:T(8,128)S(1)}, f32[4,104,128]{2,1,0:T(8,128)S(1)}, u32[]{:S(2)}, u32[]{:S(2)}) %collective-permute-start.2) | collective-permute-done | bytes 213024 | tf_op jit(solution)/shard_map/ppermute | solution.py:35
  49.9 1.3 %tile.1 = (f32[1032,128]{1,0:T(8,128)S(1)}, f32[1032,128]{1,0:T(8,128)S(1)}) custom-call(s32[3]{0:T(128)S(1)} %pad_add_fusion.where, f32[4,104,128]{2,1,0:T(8,128)S(1)} %pack_a_four.1.a0, f32[4,104,128]{2,1,0:T(8,128)S(1)} %collective-permute-done.2.a1, f32[4,2,96,128]{3,2,1,0:T(8,128)S(1)} %all-to-all-done.b_lanes), custom_call_target="tpu_custom_call" | custom-call | flops 301989888 | bytes 1875980 | tf_op jit(solution)/shard_map/tile/pallas_call | solution.py:167
  51.2 1.9 %collective-permute-start.5 = (f32[1032,128]{1,0:T(8,128)S(1)}, f32[1032,128]{1,0:T(8,128)S(1)}, u32[]{:S(2)}, u32[]{:S(2)}) collective-permute-start(f32[1032,128]{1,0:T(8,128)S(1)} %get-tuple-element.11), channel_id=1, source_target_pairs={{0,8},{1,9},{2,10},{3,11},{4,12},{5,13},{6,14},{7,15},{8,0},{9,1},... | collective-permute-start | bytes 1585160 | tf_op jit(solution)/shard_map/ppermute | solution.py:35
  53.1 1.9 %collective-permute-done.5.got = f32[1032,128]{1,0:T(8,128)S(1)} collective-permute-done((f32[1032,128]{1,0:T(8,128)S(1)}, f32[1032,128]{1,0:T(8,128)S(1)}, u32[]{:S(2)}, u32[]{:S(2)}) %collective-permute-start.5) | collective-permute-done | bytes 528416 | tf_op jit(solution)/shard_map/ppermute | solution.py:35
  55.0 0.1 scatter.1
  55.1 14.0 %all_to_all.10.came = f32[4,264,128]{2,1,0:T(8,128)S(1)} all-to-all(f32[4,264,128]{2,1,0:T(8,128)S(1)} %scatter.1), channel_id=1, replica_groups={{0,16,32,48},{1,17,33,49},{2,18,34,50},{3,19,35,51},{4,20,36,52},{5,21,..., dimensions={0} | all-to-all | bytes 1081344 | tf_op jit(solution)/shard_map/all_to_all | solution.py:306
  69.1 0.7 last.1
  (2 shorter events, 0.0 us)
Async XLA Ops:
  5.7 20.5 %collective-permute-start = (f32[104,128]{1,0:T(8,128)}, f32[104,128]{1,0:T(8,128)S(1)}, u32[]{:S(2)}, u32[]{:S(2)}) collective-permute-start(f32[104,128]{1,0:T(8,128)} %get-tuple-element.8.first), channel_id=1, source_target_pairs={{0,256},{1,257},{2,258},{3,259},{4,260},{5,261},{6,262},{7,263},{8... | collective-permute-start | bytes 159752 | tf_op jit(solution)/shard_map/ppermute | solution.py:35
  14.8 16.4 %collective-permute-start.4 = (f32[96,128]{1,0:T(8,128)}, f32[96,128]{1,0:T(8,128)S(1)}, u32[]{:S(2)}, u32[]{:S(2)}) collective-permute-start(f32[96,128]{1,0:T(8,128)} %get-tuple-element.9), channel_id=1, source_target_pairs={{0,1},{1,64},{2,128},{3,193},{4,256},{5,321},{6,384},{7,449},{8,9}... | collective-permute-start | bytes 147464 | tf_op jit(solution)/shard_map/ppermute | solution.py:35
  24.3 13.3 %collective-permute-start.3 = (f32[96,128]{1,0:T(8,128)}, f32[96,128]{1,0:T(8,128)S(1)}, u32[]{:S(2)}, u32[]{:S(2)}) collective-permute-start(f32[96,128]{1,0:T(8,128)} %get-tuple-element.9), channel_id=1, source_target_pairs={{0,0},{1,65},{2,129},{3,192},{4,257},{5,320},{6,385},{7,448},{8,8}... | collective-permute-start | bytes 147464 | tf_op jit(solution)/shard_map/ppermute | solution.py:35
  26.3 0.8 %copy-start = (f32[104,128]{1,0:T(8,128)S(1)}, f32[104,128]{1,0:T(8,128)}, u32[]{:S(2)}) copy-start(f32[104,128]{1,0:T(8,128)} %get-tuple-element.8.first) | copy-start | bytes 159748
  27.1 15.0 %collective-permute-start.1 = (f32[2,104,128]{2,1,0:T(8,128)S(1)}, f32[2,104,128]{2,1,0:T(8,128)S(1)}, u32[]{:S(2)}, u32[]{:S(2)}) collective-permute-start(f32[2,104,128]{2,1,0:T(8,128)S(1)} %pack_a_two.1.first), channel_id=1, source_target_pairs={{0,128},{1,129},{2,130},{3,131},{4,132},{5,133},{6,134},{7,135},{8... | collective-permute-start | bytes 319496 | tf_op jit(solution)/shard_map/ppermute | solution.py:35
  38.4 9.7 %all-to-all-start = ((f32[4,2,96,128]{3,2,1,0:T(8,128)}), f32[4,2,96,128]{3,2,1,0:T(8,128)S(1)}, u32[]{:S(2)}, u32[]{:S(2)}) async-start(f32[4,2,96,128]{3,2,1,0:T(8,128)} %repeat.1), calls=%async_computation | async-start | bytes 786432 | tf_op jit(solution)/shard_map/all_to_all | solution.py:286
  42.1 7.7 %collective-permute-start.2 = (f32[4,104,128]{2,1,0:T(8,128)S(1)}, f32[4,104,128]{2,1,0:T(8,128)S(1)}, u32[]{:S(2)}, u32[]{:S(2)}) collective-permute-start(f32[4,104,128]{2,1,0:T(8,128)S(1)} %pack_a_four.1.a0), channel_id=1, source_target_pairs={{0,64},{1,65},{2,66},{3,67},{4,68},{5,69},{6,70},{7,71},{8,72},{9,... | collective-permute-start | bytes 638984 | tf_op jit(solution)/shard_map/ppermute | solution.py:35
  51.2 3.8 %collective-permute-start.5 = (f32[1032,128]{1,0:T(8,128)S(1)}, f32[1032,128]{1,0:T(8,128)S(1)}, u32[]{:S(2)}, u32[]{:S(2)}) collective-permute-start(f32[1032,128]{1,0:T(8,128)S(1)} %get-tuple-element.11), channel_id=1, source_target_pairs={{0,8},{1,9},{2,10},{3,11},{4,12},{5,13},{6,14},{7,15},{8,0},{9,1},... | collective-permute-start | bytes 1585160 | tf_op jit(solution)/shard_map/ppermute | solution.py:35

commit v6 on v5

--- a/solution.py
+++ b/solution.py
@@ -90,9 +90,7 @@
         )
         for i, (first, size) in enumerate(zip(firsts, chunks))
     ]
-    small[0].start()
-    large[0].start()
-    for copy in small[1:] + large[1:]:
+    for copy in (small[1], small[2], small[0], large[0], *large[1:], *small[3:]):
         copy.start()
     small[1].wait()
     small[2].wait()

time: 70.2 us -> 70.2 us (level)
  no operation moved by 1% of the time
where the time goes in v6:
time: 70.2 us; the launch traced here: 69.8 us
  starting transfers between devices  32.2 us (46%)
  waiting for transfers between devices  14 us (20%)
  blocking collectives  14 us (20%)
  Pallas kernels  7.88 us (11%)
  local copies, waits for them, and re-layouts  0.8 us (1%)
  between operations  0.76 us (1%)
    ppermute x6, starting transfers between devices, send(): return lax.ppermute(value, AXES, pairs(move))  28.5 us
    all_to_all x1, blocking collectives, local(): came = lax.all_to_all(parts, AXES, 0, 0, axis_index_groups=x_groups())  14 us
    ppermute x6, waiting for transfers between devices, send(): return lax.ppermute(value, AXES, pairs(move))  10.1 us
    pallas_call x1, Pallas kernels, weigh_call(): pl.pallas_call(functools.partial(weigh, chunks, total), in_specs=[pl.Bloc...  5.05 us
    all_to_all x1, waiting for transfers between devices, local(): b_all = lax.all_to_all(b_own, AXES, 0, 0, axis_index_groups=y_groups())  3.87 us
    all_to_all x1, starting transfers between devices, local(): b_all = lax.all_to_all(b_own, AXES, 0, 0, axis_index_groups=y_groups())  3.76 us
    pallas_call x6, Pallas kernels, simple(): pl.pallas_call(kernel, out_shape=[jax.ShapeDtypeStruct(s, F32) for s in s...  2.84 us
  transfers between devices with their start and end apart: 7, of which 4 were waited for; matrix products, arithmetic and copies ran while one was open for 0% of the time, Pallas kernels for 1%

profile of v6, /device:TPU:104, one launch (start us, length us, event | category | flops | bytes accessed | tf_op | source)
XLA Modules:
  0.0 69.8 jit_solution(1912198321710091979)
XLA Ops:
  0.6 5.0 %weigh.1 = (f32[104,128]{1,0:T(8,128)}, f32[96,128]{1,0:T(8,128)}) custom-call(bf16[1536,1024]{1,0:T(8,128)(2,1)} %desc.1, s32[12,128]{1,0:T(8,128)} %bitcast.9, s32[1,1536]{1,0:T(1,128)} %labels.1, f32[1,24]{1,0:T(1,128)} %bitcast.12, bf16[512,1024]{1,0:T(8,128)(2,1)} %points.1, s32[1,512]{1,0:T(1,128)} %bitcast.10), custom_call_target="tpu_custom_call" | custom-call | flops 1610612736 | bytes 4194304 | tf_op jit(solution)/shard_map/weigh/pallas_call | solution.py:148
  5.7 9.1 %collective-permute-start = (f32[104,128]{1,0:T(8,128)}, f32[104,128]{1,0:T(8,128)S(1)}, u32[]{:S(2)}, u32[]{:S(2)}) collective-permute-start(f32[104,128]{1,0:T(8,128)} %get-tuple-element.8.first), channel_id=1, source_target_pairs={{0,256},{1,257},{2,258},{3,259},{4,260},{5,261},{6,262},{7,263},{8... | collective-permute-start | bytes 159752 | tf_op jit(solution)/shard_map/ppermute | solution.py:35
  14.8 9.5 %collective-permute-start.4 = (f32[96,128]{1,0:T(8,128)}, f32[96,128]{1,0:T(8,128)S(1)}, u32[]{:S(2)}, u32[]{:S(2)}) collective-permute-start(f32[96,128]{1,0:T(8,128)} %get-tuple-element.9), channel_id=1, source_target_pairs={{0,1},{1,64},{2,128},{3,193},{4,256},{5,321},{6,384},{7,449},{8,9}... | collective-permute-start | bytes 147464 | tf_op jit(solution)/shard_map/ppermute | solution.py:35
  24.3 1.9 %collective-permute-start.3 = (f32[96,128]{1,0:T(8,128)}, f32[96,128]{1,0:T(8,128)S(1)}, u32[]{:S(2)}, u32[]{:S(2)}) collective-permute-start(f32[96,128]{1,0:T(8,128)} %get-tuple-element.9), channel_id=1, source_target_pairs={{0,0},{1,65},{2,129},{3,192},{4,257},{5,320},{6,385},{7,448},{8,8}... | collective-permute-start | bytes 147464 | tf_op jit(solution)/shard_map/ppermute | solution.py:35
  26.2 0.0 collective-permute-done.second
  26.2 0.0 copy-start
  26.2 0.8 %copy-done = f32[104,128]{1,0:T(8,128)S(1)} copy-done((f32[104,128]{1,0:T(8,128)S(1)}, f32[104,128]{1,0:T(8,128)}, u32[]{:S(2)}) %copy-start) | copy-done | bytes 53272
  27.1 4.1 %collective-permute-start.1 = (f32[2,104,128]{2,1,0:T(8,128)S(1)}, f32[2,104,128]{2,1,0:T(8,128)S(1)}, u32[]{:S(2)}, u32[]{:S(2)}) collective-permute-start(f32[2,104,128]{2,1,0:T(8,128)S(1)} %pack_a_two.1.first), channel_id=1, source_target_pairs={{0,128},{1,129},{2,130},{3,131},{4,132},{5,133},{6,134},{7,135},{8... | collective-permute-start | bytes 319496 | tf_op jit(solution)/shard_map/ppermute | solution.py:35
  31.2 0.0 collective-permute-done.4.second
  31.2 6.4 %collective-permute-done.3.first = f32[96,128]{1,0:T(8,128)S(1)} collective-permute-done((f32[96,128]{1,0:T(8,128)}, f32[96,128]{1,0:T(8,128)S(1)}, u32[]{:S(2)}, u32[]{:S(2)}) %collective-permute-start.3) | collective-permute-done | bytes 49184 | tf_op jit(solution)/shard_map/ppermute | solution.py:35
  37.6 0.8 %repeat.1 = f32[4,2,96,128]{3,2,1,0:T(8,128)} custom-call(f32[96,128]{1,0:T(8,128)S(1)} %collective-permute-done.3.first, f32[96,128]{1,0:T(8,128)S(1)} %collective-permute-done.4.second), custom_call_target="tpu_custom_call" | custom-call | bytes 491520 | tf_op jit(solution)/shard_map/repeat/pallas_call | solution.py:165
  38.3 3.8 %all-to-all-start = ((f32[4,2,96,128]{3,2,1,0:T(8,128)}), f32[4,2,96,128]{3,2,1,0:T(8,128)S(1)}, u32[]{:S(2)}, u32[]{:S(2)}) async-start(f32[4,2,96,128]{3,2,1,0:T(8,128)} %repeat.1), calls=%async_computation | async-start | bytes 786432 | tf_op jit(solution)/shard_map/all_to_all | solution.py:284
  42.1 0.0 collective-permute-done.1.second
  42.1 1.9 %collective-permute-start.2 = (f32[4,104,128]{2,1,0:T(8,128)S(1)}, f32[4,104,128]{2,1,0:T(8,128)S(1)}, u32[]{:S(2)}, u32[]{:S(2)}) collective-permute-start(f32[4,104,128]{2,1,0:T(8,128)S(1)} %pack_a_four.1.a0), channel_id=1, source_target_pairs={{0,64},{1,65},{2,66},{3,67},{4,68},{5,69},{6,70},{7,71},{8,72},{9,... | collective-permute-start | bytes 638984 | tf_op jit(solution)/shard_map/ppermute | solution.py:35
  44.1 0.1 pad_add_fusion.where
  44.2 3.9 %all-to-all-done.b_lanes = f32[4,2,96,128]{3,2,1,0:T(8,128)S(1)} async-done(((f32[4,2,96,128]{3,2,1,0:T(8,128)}), f32[4,2,96,128]{3,2,1,0:T(8,128)S(1)}, u32[]{:S(2)}, u32[]{:S(2)}) %all-to-all-start) | async-done | bytes 393248 | tf_op jit(solution)/shard_map/all_to_all | solution.py:284
  48.0 1.8 %collective-permute-done.2.a1 = f32[4,104,128]{2,1,0:T(8,128)S(1)} collective-permute-done((f32[4,104,128]{2,1,0:T(8,128)S(1)}, f32[4,104,128]{2,1,0:T(8,128)S(1)}, u32[]{:S(2)}, u32[]{:S(2)}) %collective-permute-start.2) | collective-permute-done | bytes 213024 | tf_op jit(solution)/shard_map/ppermute | solution.py:35
  49.9 1.3 %tile.1 = (f32[1032,128]{1,0:T(8,128)S(1)}, f32[1032,128]{1,0:T(8,128)S(1)}) custom-call(s32[3]{0:T(128)S(1)} %pad_add_fusion.where, f32[4,104,128]{2,1,0:T(8,128)S(1)} %pack_a_four.1.a0, f32[4,104,128]{2,1,0:T(8,128)S(1)} %collective-permute-done.2.a1, f32[4,2,96,128]{3,2,1,0:T(8,128)S(1)} %all-to-all-done.b_lanes), custom_call_target="tpu_custom_call" | custom-call | flops 301989888 | bytes 1875980 | tf_op jit(solution)/shard_map/tile/pallas_call | solution.py:165
  51.2 1.9 %collective-permute-start.5 = (f32[1032,128]{1,0:T(8,128)S(1)}, f32[1032,128]{1,0:T(8,128)S(1)}, u32[]{:S(2)}, u32[]{:S(2)}) collective-permute-start(f32[1032,128]{1,0:T(8,128)S(1)} %get-tuple-element.11), channel_id=1, source_target_pairs={{0,8},{1,9},{2,10},{3,11},{4,12},{5,13},{6,14},{7,15},{8,0},{9,1},... | collective-permute-start | bytes 1585160 | tf_op jit(solution)/shard_map/ppermute | solution.py:35
  53.1 1.9 %collective-permute-done.5.got = f32[1032,128]{1,0:T(8,128)S(1)} collective-permute-done((f32[1032,128]{1,0:T(8,128)S(1)}, f32[1032,128]{1,0:T(8,128)S(1)}, u32[]{:S(2)}, u32[]{:S(2)}) %collective-permute-start.5) | collective-permute-done | bytes 528416 | tf_op jit(solution)/shard_map/ppermute | solution.py:35
  55.0 0.1 scatter.1
  55.0 14.0 %all_to_all.10.came = f32[4,264,128]{2,1,0:T(8,128)S(1)} all-to-all(f32[4,264,128]{2,1,0:T(8,128)S(1)} %scatter.1), channel_id=1, replica_groups={{0,16,32,48},{1,17,33,49},{2,18,34,50},{3,19,35,51},{4,20,36,52},{5,21,..., dimensions={0} | all-to-all | bytes 1081344 | tf_op jit(solution)/shard_map/all_to_all | solution.py:304
  69.1 0.7 last.1
  (2 shorter events, 0.0 us)
Async XLA Ops:
  5.7 20.5 %collective-permute-start = (f32[104,128]{1,0:T(8,128)}, f32[104,128]{1,0:T(8,128)S(1)}, u32[]{:S(2)}, u32[]{:S(2)}) collective-permute-start(f32[104,128]{1,0:T(8,128)} %get-tuple-element.8.first), channel_id=1, source_target_pairs={{0,256},{1,257},{2,258},{3,259},{4,260},{5,261},{6,262},{7,263},{8... | collective-permute-start | bytes 159752 | tf_op jit(solution)/shard_map/ppermute | solution.py:35
  14.8 16.4 %collective-permute-start.4 = (f32[96,128]{1,0:T(8,128)}, f32[96,128]{1,0:T(8,128)S(1)}, u32[]{:S(2)}, u32[]{:S(2)}) collective-permute-start(f32[96,128]{1,0:T(8,128)} %get-tuple-element.9), channel_id=1, source_target_pairs={{0,1},{1,64},{2,128},{3,193},{4,256},{5,321},{6,384},{7,449},{8,9}... | collective-permute-start | bytes 147464 | tf_op jit(solution)/shard_map/ppermute | solution.py:35
  24.3 13.3 %collective-permute-start.3 = (f32[96,128]{1,0:T(8,128)}, f32[96,128]{1,0:T(8,128)S(1)}, u32[]{:S(2)}, u32[]{:S(2)}) collective-permute-start(f32[96,128]{1,0:T(8,128)} %get-tuple-element.9), channel_id=1, source_target_pairs={{0,0},{1,65},{2,129},{3,192},{4,257},{5,320},{6,385},{7,448},{8,8}... | collective-permute-start | bytes 147464 | tf_op jit(solution)/shard_map/ppermute | solution.py:35
  26.2 0.8 %copy-start = (f32[104,128]{1,0:T(8,128)S(1)}, f32[104,128]{1,0:T(8,128)}, u32[]{:S(2)}) copy-start(f32[104,128]{1,0:T(8,128)} %get-tuple-element.8.first) | copy-start | bytes 159748
  27.1 15.0 %collective-permute-start.1 = (f32[2,104,128]{2,1,0:T(8,128)S(1)}, f32[2,104,128]{2,1,0:T(8,128)S(1)}, u32[]{:S(2)}, u32[]{:S(2)}) collective-permute-start(f32[2,104,128]{2,1,0:T(8,128)S(1)} %pack_a_two.1.first), channel_id=1, source_target_pairs={{0,128},{1,129},{2,130},{3,131},{4,132},{5,133},{6,134},{7,135},{8... | collective-permute-start | bytes 319496 | tf_op jit(solution)/shard_map/ppermute | solution.py:35
  38.3 9.7 %all-to-all-start = ((f32[4,2,96,128]{3,2,1,0:T(8,128)}), f32[4,2,96,128]{3,2,1,0:T(8,128)S(1)}, u32[]{:S(2)}, u32[]{:S(2)}) async-start(f32[4,2,96,128]{3,2,1,0:T(8,128)} %repeat.1), calls=%async_computation | async-start | bytes 786432 | tf_op jit(solution)/shard_map/all_to_all | solution.py:284
  42.1 7.7 %collective-permute-start.2 = (f32[4,104,128]{2,1,0:T(8,128)S(1)}, f32[4,104,128]{2,1,0:T(8,128)S(1)}, u32[]{:S(2)}, u32[]{:S(2)}) collective-permute-start(f32[4,104,128]{2,1,0:T(8,128)S(1)} %pack_a_four.1.a0), channel_id=1, source_target_pairs={{0,64},{1,65},{2,66},{3,67},{4,68},{5,69},{6,70},{7,71},{8,72},{9,... | collective-permute-start | bytes 638984 | tf_op jit(solution)/shard_map/ppermute | solution.py:35
  51.2 3.8 %collective-permute-start.5 = (f32[1032,128]{1,0:T(8,128)S(1)}, f32[1032,128]{1,0:T(8,128)S(1)}, u32[]{:S(2)}, u32[]{:S(2)}) collective-permute-start(f32[1032,128]{1,0:T(8,128)S(1)} %get-tuple-element.11), channel_id=1, source_target_pairs={{0,8},{1,9},{2,10},{3,11},{4,12},{5,13},{6,14},{7,15},{8,0},{9,1},... | collective-permute-start | bytes 1585160 | tf_op jit(solution)/shard_map/ppermute | solution.py:35
